TPU v7x, 32 devices: a whole 2x2x4 slice. The times are simulated.
32 devices in a mesh: seq: 8 (over z, x), fsdp: 4 (over y, core).
Axes of the slice: x: 2, y: 2, z: 4, core: 2. Of those that a mesh axis runs over, the one named last changes fastest.
Arguments:
- tokens: bfloat16 [4, 4096, 1024], P('fsdp', 'seq'), may hold values from -6 to 6
- cotangent: bfloat16 [4, 4096, 1024], P('fsdp', 'seq'), may hold values from -6 to 6
- chosen: int32 [4, 512], P('fsdp', 'seq'), may hold values from 0 to 511, as said below
- positions: int32 [4, 4096], P('fsdp', 'seq'), may hold values from 0 to 4095, as said below
- lengths: int32 [4, 3], P('fsdp'), may hold values from 1 to 2048, 4096 in all within a row
- w_qkv: float32 [1024, 3072], P(('seq', 'fsdp')), may hold values from -0.09375 to 0.09375
- m_qkv: float32 [1024, 3072], P(('seq', 'fsdp')), may hold values from -0.00018310547 to 0.00018310547
- v_qkv: float32 [1024, 3072], P(('seq', 'fsdp')), may hold values from 4.178572e-09 to 1.6722232e-08
- w_out: float32 [1024, 1024], P(('seq', 'fsdp')), may hold values from -0.5 to 0.5
- m_out: float32 [1024, 1024], P(('seq', 'fsdp')), may hold values from -0.00018310547 to 0.00018310547
- v_out: float32 [1024, 1024], P(('seq', 'fsdp')), may hold values from 4.178572e-09 to 1.6722232e-08
- w_up: float32 [1024, 4096], P(('seq', 'fsdp')), may hold values from -0.1875 to 0.1875
- m_up: float32 [1024, 4096], P(('seq', 'fsdp')), may hold values from -0.00018310547 to 0.00018310547
- v_up: float32 [1024, 4096], P(('seq', 'fsdp')), may hold values from 4.178572e-09 to 1.6722232e-08
- w_down: float32 [4096, 1024], P(('seq', 'fsdp')), may hold values from -0.09375 to 0.09375
- m_down: float32 [4096, 1024], P(('seq', 'fsdp')), may hold values from -0.00018310547 to 0.00018310547
- v_down: float32 [4096, 1024], P(('seq', 'fsdp')), may hold values from 4.178572e-09 to 1.6722232e-08
- vectors: float32 [1024, 5], P(('seq', 'fsdp'))
- m_vec: float32 [1024, 5], P(('seq', 'fsdp')), may hold values from -0.0007324219 to 0.0007324219
- v_vec: float32 [1024, 5], P(('seq', 'fsdp')), may hold values from 6.688893e-08 to 2.677146e-07
Outputs:
- mixed: bfloat16 [4, 4096, 1024], P('fsdp', 'seq')
- grad_tokens: bfloat16 [4, 4096, 1024], P('fsdp', 'seq')
- first_qkv: float32 [1024, 3072], P(('seq', 'fsdp'))
- second_qkv: float32 [1024, 3072], P(('seq', 'fsdp'))
- new_qkv: float32 [1024, 3072], P(('seq', 'fsdp'))
- first_out: float32 [1024, 1024], P(('seq', 'fsdp'))
- second_out: float32 [1024, 1024], P(('seq', 'fsdp'))
- new_out: float32 [1024, 1024], P(('seq', 'fsdp'))
- first_up: float32 [1024, 4096], P(('seq', 'fsdp'))
- second_up: float32 [1024, 4096], P(('seq', 'fsdp'))
- new_up: float32 [1024, 4096], P(('seq', 'fsdp'))
- first_down: float32 [4096, 1024], P(('seq', 'fsdp'))
- second_down: float32 [4096, 1024], P(('seq', 'fsdp'))
- new_down: float32 [4096, 1024], P(('seq', 'fsdp'))
- first_vec: float32 [1024, 5], P(('seq', 'fsdp'))
- second_vec: float32 [1024, 5], P(('seq', 'fsdp'))
- new_vec: float32 [1024, 5], P(('seq', 'fsdp'))
- grad_norm: float32 [], replicated
Inputs may be any that keep to these rules, and one draw needn't show every extreme that they name: `chosen`: in each batch, the 64 entries of one index of seq are distinct row numbers of that device's 512 rows. Each batch's row holds every number of 0 to 4095 once. In each run of 128 numbers starting at a multiple of it, one index of seq takes exactly one aligned run of 16 consecutive numbers, and its positions rise along its rows. Each batch's lengths sum to 4096.
All inputs are finite; a program needn't handle non-finite values.
Results may differ from a plain program's by a relative error of at most 0.015.
The roundings to bfloat16 on the way count: a program that leaves them out, or rounds other values in their place, can miss the bound.
Values may be sent and summed in bfloat16 or wider, within the bound.
No kernel may reach another device: no remote copies, remote signals or barrier semaphores. Data moves between devices by JAX's collectives and lax.ppermute only.
A program may use at most 256 MiB of HBM per device.

v0:
```python
import math

import jax
import jax.numpy as jnp
from jax import lax
from jax.experimental import pallas as pl
from jax.experimental.pallas import tpu as pltpu
from jax.sharding import PartitionSpec as P

HEADS = 16
STEP = 10


HIGHEST = lax.Precision.HIGHEST
RATES = (0.01, 0.05, 0.02, 0.01, 1.0)
BETA_ONE = 0.9
BETA_TWO = 0.95
ADAM_EPS = 1e-08
DECAY_RATE = 0.1
CLIP_NORM = 1.0
NORM_EPS = 1e-05
MASKED = -1e30
LOW = jnp.bfloat16
FULL = jnp.float32


def normalize(values):
    centre = values - jnp.mean(values, axis=-1, keepdims=True)
    inverse = lax.rsqrt(jnp.mean(centre * centre, axis=-1, keepdims=True) + NORM_EPS)
    return (centre * inverse, inverse)


def norm_back(normed, inverse, grad_normed):
    mean_grad = jnp.mean(grad_normed, axis=-1, keepdims=True)
    mean_cross = jnp.mean(grad_normed * normed, axis=-1, keepdims=True)
    return inverse * (grad_normed - mean_grad - normed * mean_cross)


def gelu_tanh(values):
    return jax.nn.gelu(values, approximate=True)


def segment_of(places, seq_ends):
    return jnp.sum((places[:, None] >= seq_ends[None, :]).astype(jnp.int32), axis=1)


def scores_for(query, key_block, query_place, query_seg, key_place, key_seg):
    raw = jnp.einsum("qhd,khd->qhk", query, key_block, preferred_element_type=jnp.float32) * 0.125
    allowed = (query_seg[:, None] == key_seg[None, :]) & (
        key_place[None, :] <= query_place[:, None]
    )
    return (raw, allowed[:, None, :])


def block_grads(
    query,
    grad_heads,
    log_total,
    delta,
    query_place,
    query_seg,
    key_block,
    value_block,
    key_place,
    key_seg,
):
    raw, allowed = scores_for(query, key_block, query_place, query_seg, key_place, key_seg)
    probs = jnp.where(allowed, jnp.exp(raw - log_total[..., None]), 0.0)
    grad_probs = jnp.einsum(
        "qhd,khd->qhk", grad_heads, value_block, preferred_element_type=jnp.float32
    )
    grad_scores = (probs * (grad_probs - delta[..., None])).astype(jnp.bfloat16)
    return (probs, grad_scores)


def adam_step(weight, first, second, grad, factor, rate):
    clipped = grad * factor
    first_new = BETA_ONE * first + (1.0 - BETA_ONE) * clipped
    second_new = BETA_TWO * second + (1.0 - BETA_TWO) * clipped * clipped
    first_hat = first_new / (1.0 - BETA_ONE**STEP)
    second_hat = second_new / (1.0 - BETA_TWO**STEP)
    weight_new = weight - rate * (
        first_hat / (jnp.sqrt(second_hat) + ADAM_EPS) + DECAY_RATE * weight
    )
    return (first_new, second_new, weight_new)


def body_general(
    tokens,
    cotangent,
    chosen,
    positions,
    lengths,
    w_qkv,
    m_qkv,
    v_qkv,
    w_out,
    m_out,
    v_out,
    w_up,
    m_up,
    v_up,
    w_down,
    m_down,
    v_down,
    vectors,
    m_vec,
    v_vec,
):
    width = tokens.shape[2]
    heads = HEADS
    head_size = width // heads
    rows = chosen[0]
    local_rows = tokens[0]
    routed = rows.shape[0]
    seq_ends = jnp.cumsum(lengths[0])
    query_place = jnp.take(positions[0], rows)
    query_seg = segment_of(query_place, seq_ends)
    gathered_weights = (
        lax.all_gather(w_qkv.astype(jnp.bfloat16), ("seq", "fsdp"), axis=0, tiled=True),
        lax.all_gather(w_out.astype(jnp.bfloat16), ("seq", "fsdp"), axis=0, tiled=True),
        lax.all_gather(w_up.astype(jnp.bfloat16), ("seq", "fsdp"), axis=0, tiled=True),
        lax.all_gather(w_down.astype(jnp.bfloat16), ("seq", "fsdp"), axis=0, tiled=True),
        lax.all_gather(vectors.astype(jnp.bfloat16), ("seq", "fsdp"), axis=0, tiled=True),
    )
    weight_qkv, weight_out, weight_up, weight_down, vec_low = gathered_weights
    params = vec_low.astype(jnp.float32)
    gain_one, shift_one, gain_two, shift_two = (
        params[:, 0],
        params[:, 1],
        params[:, 2],
        params[:, 3],
    )
    route_vec = params[:, 4]
    picked = jnp.take(local_rows, rows, axis=0)
    inputs = picked.astype(jnp.float32)
    normed_one, inverse_one = normalize(inputs)
    input_one = (normed_one * gain_one + shift_one).astype(jnp.bfloat16)
    joined = jnp.dot(input_one, weight_qkv, preferred_element_type=jnp.float32).astype(jnp.bfloat16)
    query = joined[:, :width].reshape(routed, heads, head_size)
    key_value = joined[:, width:]
    gathered_kv = lax.all_gather(key_value, "seq", axis=0, tiled=True)
    key_place = lax.all_gather(query_place, "seq", axis=0, tiled=True)
    key_seg = segment_of(key_place, seq_ends)
    total_keys = gathered_kv.shape[0]
    key_width = min(512, total_keys)
    key_blocks = total_keys // key_width

    def split_blocks(kv_rows):
        return kv_rows.reshape(key_blocks, key_width, 2, heads, head_size)

    place_blocks = key_place.reshape(key_blocks, key_width)
    seg_blocks = key_seg.reshape(key_blocks, key_width)

    def stats_step(carry, block):
        row_max, row_total = carry
        kv_block, block_place, block_seg = block
        raw, allowed = scores_for(
            query, kv_block[:, 0], query_place, query_seg, block_place, block_seg
        )
        masked = jnp.where(allowed, raw, MASKED)
        new_max = jnp.maximum(row_max, jnp.max(masked, axis=-1))
        expo = jnp.where(allowed, jnp.exp(masked - new_max[..., None]), 0.0)
        new_total = row_total * jnp.exp(row_max - new_max) + jnp.sum(expo, axis=-1)
        return ((new_max, new_total), None)

    start_max = jnp.full((routed, heads), MASKED, jnp.float32)
    start_total = jnp.zeros((routed, heads), jnp.float32)
    (row_max, row_total), _ = lax.scan(
        stats_step, (start_max, start_total), (split_blocks(gathered_kv), place_blocks, seg_blocks)
    )
    log_total = row_max + jnp.log(row_total)

    def probs_for(key_block, block_place, block_seg):
        raw, allowed = scores_for(query, key_block, query_place, query_seg, block_place, block_seg)
        return jnp.where(allowed, jnp.exp(raw - log_total[..., None]), 0.0)

    def output_step(carry, block):
        rounded_sum, rest_sum = carry
        kv_block, block_place, block_seg = block
        probs = probs_for(kv_block[:, 0], block_place, block_seg)
        value_block = kv_block[:, 1]
        probs_high = probs.astype(jnp.bfloat16)
        probs_rest = (probs - probs_high.astype(jnp.float32)).astype(jnp.bfloat16)
        rounded_sum = rounded_sum + jnp.einsum(
            "qhk,khd->qhd", probs_high, value_block, preferred_element_type=jnp.float32
        )
        rest_sum = rest_sum + jnp.einsum(
            "qhk,khd->qhd", probs_rest, value_block, preferred_element_type=jnp.float32
        )
        return ((rounded_sum, rest_sum), None)

    start_out = jnp.zeros((routed, heads, head_size), jnp.float32)
    (attended, attended_rest), _ = lax.scan(
        output_step, (start_out, start_out), (split_blocks(gathered_kv), place_blocks, seg_blocks)
    )
    attended_exact = attended + attended_rest
    attended_low = attended.reshape(routed, width).astype(jnp.bfloat16)
    branch_attn = jnp.dot(attended_low, weight_out, preferred_element_type=jnp.float32)
    middle = inputs + branch_attn
    normed_two, inverse_two = normalize(middle)
    input_two = (normed_two * gain_two + shift_two).astype(jnp.bfloat16)
    hidden = jnp.dot(input_two, weight_up, preferred_element_type=jnp.float32)
    activated = gelu_tanh(hidden).astype(jnp.bfloat16)
    branch_mlp = jnp.dot(activated, weight_down, preferred_element_type=jnp.float32)
    gate = jax.nn.sigmoid(jnp.dot(picked, vec_low[:, 4], preferred_element_type=jnp.float32))
    branches = branch_attn + branch_mlp
    result = inputs + gate[:, None] * branches
    mixed = local_rows.at[rows].set(result.astype(jnp.bfloat16))[None]
    back_rows = cotangent[0]
    grad_result = jnp.take(back_rows, rows, axis=0).astype(jnp.float32)
    grad_logit = jnp.sum(grad_result * branches, axis=-1) * gate * (1.0 - gate)
    grad_branch = gate[:, None] * grad_result
    grad_mlp = grad_branch.astype(jnp.bfloat16)
    grad_w_down = jnp.dot(activated.T, grad_mlp, preferred_element_type=jnp.float32)
    grad_act = jnp.dot(grad_mlp, weight_down.T, preferred_element_type=jnp.float32)
    _, gelu_pull = jax.vjp(gelu_tanh, hidden)
    grad_hidden = gelu_pull(grad_act)[0].astype(jnp.bfloat16)
    grad_w_up = jnp.dot(input_two.T, grad_hidden, preferred_element_type=jnp.float32)
    grad_two = jnp.dot(grad_hidden, weight_up.T, preferred_element_type=jnp.float32)
    grad_gain_two = jnp.sum(grad_two * normed_two, axis=0)
    grad_shift_two = jnp.sum(grad_two, axis=0)
    grad_middle = norm_back(normed_two, inverse_two, grad_two * gain_two)
    grad_attn = (grad_branch + grad_middle).astype(jnp.bfloat16)
    grad_w_out = jnp.dot(attended_low.T, grad_attn, preferred_element_type=jnp.float32)
    grad_heads = jnp.dot(grad_attn, weight_out.T, preferred_element_type=jnp.float32).astype(
        jnp.bfloat16
    )
    grad_heads = grad_heads.reshape(routed, heads, head_size)
    delta = jnp.sum(grad_heads.astype(jnp.float32) * attended_exact, axis=-1)

    def query_step(carry, block):
        kv_block, block_place, block_seg = block
        _, grad_scores = block_grads(
            query,
            grad_heads,
            log_total,
            delta,
            query_place,
            query_seg,
            kv_block[:, 0],
            kv_block[:, 1],
            block_place,
            block_seg,
        )
        carry = carry + jnp.einsum(
            "qhk,khd->qhd", grad_scores, kv_block[:, 0], preferred_element_type=jnp.float32
        )
        return (carry, None)

    grad_query, _ = lax.scan(
        query_step, start_out, (split_blocks(gathered_kv), place_blocks, seg_blocks)
    )
    grad_query = grad_query.reshape(routed, width) * 0.125
    piece_rows = math.gcd(routed * lax.axis_size("seq"), 512)
    pieces = routed * lax.axis_size("seq") // piece_rows

    def piece_term(piece_index):
        piece_start = piece_index * piece_rows
        kv_piece = lax.dynamic_slice_in_dim(gathered_kv, piece_start, piece_rows, 0).reshape(
            piece_rows, 2, heads, head_size
        )
        piece_place = lax.dynamic_slice_in_dim(key_place, piece_start, piece_rows, 0)
        piece_seg = lax.dynamic_slice_in_dim(key_seg, piece_start, piece_rows, 0)
        probs, grad_scores = block_grads(
            query,
            grad_heads,
            log_total,
            delta,
            query_place,
            query_seg,
            kv_piece[:, 0],
            kv_piece[:, 1],
            piece_place,
            piece_seg,
        )
        grad_keys = (
            jnp.einsum("qhk,qhd->khd", grad_scores, query, preferred_element_type=jnp.float32)
            * 0.125
        )
        grad_values = jnp.einsum(
            "qhk,qhd->khd",
            probs.astype(jnp.bfloat16),
            grad_heads,
            preferred_element_type=jnp.float32,
        )
        return jnp.concatenate(
            [grad_keys.reshape(piece_rows, width), grad_values.reshape(piece_rows, width)], axis=1
        )

    terms = lax.map(piece_term, jnp.arange(pieces, dtype=jnp.int32))
    grad_key_value = lax.psum_scatter(
        terms.reshape(routed * lax.axis_size("seq"), 2 * width),
        "seq",
        scatter_dimension=0,
        tiled=True,
    )
    grad_joined = jnp.concatenate([grad_query, grad_key_value], axis=1).astype(jnp.bfloat16)
    grad_w_qkv = jnp.dot(input_one.T, grad_joined, preferred_element_type=jnp.float32)
    grad_one = jnp.dot(grad_joined, weight_qkv.T, preferred_element_type=jnp.float32)
    grad_gain_one = jnp.sum(grad_one * normed_one, axis=0)
    grad_shift_one = jnp.sum(grad_one, axis=0)
    grad_route = jnp.dot(grad_logit, inputs, precision=HIGHEST)
    grad_inputs = (
        grad_result
        + grad_middle
        + norm_back(normed_one, inverse_one, grad_one * gain_one)
        + grad_logit[:, None] * route_vec
    )
    grad_tokens = back_rows.at[rows].set(grad_inputs.astype(jnp.bfloat16))[None]
    grad_vec = jnp.stack(
        [grad_gain_one, grad_shift_one, grad_gain_two, grad_shift_two, grad_route], axis=1
    )
    local_grads = (grad_w_qkv, grad_w_out, grad_w_up, grad_w_down, grad_vec)
    shards = (
        lax.psum_scatter(local_grads[0], ("seq", "fsdp"), scatter_dimension=0, tiled=True),
        lax.psum_scatter(local_grads[1], ("seq", "fsdp"), scatter_dimension=0, tiled=True),
        lax.psum_scatter(local_grads[2], ("seq", "fsdp"), scatter_dimension=0, tiled=True),
        lax.psum_scatter(local_grads[3], ("seq", "fsdp"), scatter_dimension=0, tiled=True),
        lax.psum_scatter(local_grads[4], ("seq", "fsdp"), scatter_dimension=0, tiled=True),
    )
    local_squares = sum((jnp.sum(shard * shard) for shard in shards))
    grad_norm = jnp.sqrt(lax.psum(local_squares, ("seq", "fsdp")))
    factor = CLIP_NORM / jnp.maximum(grad_norm, CLIP_NORM)
    masters = (w_qkv, w_out, w_up, w_down, vectors)
    firsts = (m_qkv, m_out, m_up, m_down, m_vec)
    seconds = (v_qkv, v_out, v_up, v_down, v_vec)
    updates = [
        adam_step(masters[kind], firsts[kind], seconds[kind], shards[kind], factor, RATES[kind])
        for kind in range(5)
    ]
    return (
        mixed,
        grad_tokens,
        updates[0][0],
        updates[0][1],
        updates[0][2],
        updates[1][0],
        updates[1][1],
        updates[1][2],
        updates[2][0],
        updates[2][1],
        updates[2][2],
        updates[3][0],
        updates[3][1],
        updates[3][2],
        updates[4][0],
        updates[4][1],
        updates[4][2],
        grad_norm,
    )


HBM = pl.BlockSpec(memory_space=pltpu.HBM)
VMEM = pl.BlockSpec(memory_space=pltpu.VMEM)
ANY = pl.BlockSpec(memory_space=pl.ANY)
SMEM = pl.BlockSpec(memory_space=pltpu.SMEM)


def struct(shape, dtype):
    return jax.ShapeDtypeStruct(shape, dtype)


class Source:
    def __init__(self, ref, semaphore):
        self.ref, self.semaphore = ref, semaphore

    def start(self, into, part=None):
        source = self.ref if part is None else self.ref.at[part]
        self.into, self.ready = into, False
        self.copy = pltpu.make_async_copy(source, into, self.semaphore)
        self.copy.start()

    def get(self):
        if not self.ready:
            self.copy.wait()
            self.ready = True
        return self.into


class Target:
    def __init__(self, ref, stage, semaphore):
        self.ref, self.semaphore = stage, semaphore
        self.copy = pltpu.make_async_copy(stage, ref, semaphore)
        self.sent = False

    def send(self):
        self.copy.start()
        self.sent = True


class Sink:
    def __init__(self, shape, parts):
        self.shape, self.dtype, self.parts = shape.shape, shape.dtype, parts


class Parts:
    def __init__(self, ref, semaphores):
        self.ref, self.semaphores, self.copies = ref, semaphores, []

    def put(self, source, part=None):
        into = self.ref if part is None else self.ref.at[part]
        semaphore = self.semaphores[len(self.copies)]
        self.copies.append(pltpu.make_async_copy(source, into, semaphore))
        self.copies[-1].start()


class Raw:
    def __init__(self, array):
        self.array = array


class Near(Raw):
    pass


class Held:
    def __init__(self, ref):
        self.ref = ref

    def get(self):
        return self.ref


def local_call(body, out_shape, scalars, arrays, scratch=(), wait=(), spare=4):
    near = [isinstance(array, Near) for array in arrays]
    by_parts = [isinstance(out, Sink) for out in out_shape]
    others = [
        pltpu.with_memory_space_constraint(other.array, pltpu.HBM)
        if isinstance(other, Raw)
        else other
        for other in wait
    ]
    lanes, places = 0, []
    for out in out_shape:
        places.append(lanes)
        lanes += out.parts if isinstance(out, Sink) else 1
    staged = [not isinstance(array, Raw) for array in arrays]
    arrays = [array if stage else array.array for array, stage in zip(arrays, staged)]
    placed = [
        array if beside else pltpu.with_memory_space_constraint(array, pltpu.HBM)
        for array, beside in zip(arrays, near)
    ]
    sizes = (len(scalars), len(arrays), len(wait), len(out_shape), sum(staged), by_parts.count(False))

    def kernel(*refs):
        groups, at = [], 0
        for size in sizes:
            groups.append(refs[at : at + size])
            at += size
        values, ins, _, outs, stage_in, stage_out = groups
        extra, (sem_in, sem_out) = refs[at:-2], refs[-2:]
        sources = [
            Held(ref) if beside else Source(ref, sem_in.at[i])
            for i, (ref, beside) in enumerate(zip(ins, near))
        ]
        stages = iter(stage_in)
        for source, stage in zip(sources, staged):
            if stage:
                source.start(next(stages))
        stages = iter(stage_out)
        targets = []
        for ref, out, split, place in zip(outs, out_shape, by_parts, places):
            if split:
                targets.append(Parts(ref, [sem_out.at[place + i] for i in range(out.parts)]))
            else:
                targets.append(Target(ref, next(stages), sem_out.at[place]))
        body(*values, *sources, *targets, *extra)
        for target, split in zip(targets, by_parts):
            if not split and not target.sent:
                target.send()
        for target, split in zip(targets, by_parts):
            for copy in target.copies if split else [target.copy]:
                copy.wait()

    stages = [
        pltpu.VMEM(array.shape, array.dtype) for array, stage in zip(arrays, staged) if stage
    ]
    stages += [
        pltpu.VMEM(out.shape, out.dtype) for out, split in zip(out_shape, by_parts) if not split
    ]
    areas = (*stages, *scratch, *(array for array, beside in zip(arrays, near) if beside))
    held = sum(math.prod(area.shape) * area.dtype.itemsize for area in areas)
    return pl.pallas_call(
        kernel,
        out_shape=[pltpu.HBM(out.shape, out.dtype) for out in out_shape],
        in_specs=[
            *[SMEM] * len(scalars),
            *(VMEM if beside else HBM for beside in near),
            *(HBM if isinstance(other, Raw) else ANY for other in wait),
        ],
        out_specs=[HBM] * len(out_shape),
        scratch_shapes=[
            *stages,
            *scratch,
            pltpu.SemaphoreType.DMA((len(arrays),)),
            pltpu.SemaphoreType.DMA((lanes,)),
        ],
        compiler_params=pltpu.CompilerParams(vmem_limit_bytes=held + spare * 1024 * 1024),
        cost_estimate=pl.CostEstimate(flops=1024, bytes_accessed=1024, transcendentals=0),
    )(*scalars, *placed, *others)


def mul(left, right):
    return jnp.dot(left, right, preferred_element_type=FULL)


def mul_right_t(left, right):
    return lax.dot_general(left, right, (((1,), (1,)), ((), ())), preferred_element_type=FULL)


def mul_left_t(left, right):
    return lax.dot_general(left, right, (((0,), (0,)), ((), ())), preferred_element_type=FULL)


def one_hot_columns(chosen, held):
    rows = lax.broadcasted_iota(jnp.int32, (held, chosen.shape[1]), 0)
    return (rows == chosen).astype(FULL)


def rows_of(blocks):
    return blocks.reshape(blocks.shape[0] * blocks.shape[1], blocks.shape[2])


def gelu_both(values):
    square = values * values
    inner = 0.7978845608028654 * values * (1.0 + 0.044715 * square)
    bend = jnp.tanh(inner)
    half = 0.5 * (1.0 + bend)
    slope = 0.7978845608028654 * (1.0 + 0.134145 * square)
    return values * half, half + 0.5 * values * (1.0 - bend * bend) * slope


def gate_of(inputs, params):
    return jax.nn.sigmoid(jnp.sum(inputs * params[4:5], axis=-1, keepdims=True))


def pack_rows_body(chosen, tokens, own_x, copies):
    picker = one_hot_columns(chosen.get()[...], tokens.ref.shape[0]).astype(LOW)
    own = mul_left_t(picker, tokens.get()[...]).astype(LOW)
    own_x.ref[...] = own
    for seat in range(copies.ref.shape[0]):
        copies.ref[seat] = own


def pack_first_body(chosen, positions, w_qkv, vectors, first, side, turn):
    count, shard, wide = first.ref.shape
    span = (wide - 128) // 3
    width = span * count
    picks = chosen.get()[...]
    routed = picks.shape[1]
    picker = one_hot_columns(picks, positions.ref.shape[1]).astype(LOW)
    place = positions.get()[...]
    line = lax.broadcasted_iota(jnp.int32, (16, place.shape[1]), 0)
    place = jnp.where(line == 0, place >> 8, place & 255).astype(FULL).astype(LOW)
    turn[...] = jnp.zeros_like(turn)
    turn[0:5, 0:shard] = vectors.get()[...]
    side[...] = jnp.transpose(turn[...])[0:shard]
    side[0:16, 128 - routed :] = mul(place, picker)
    extra = side[...].astype(LOW)
    weights = w_qkv.get()
    for seat in range(count):
        for part in range(3):
            columns = slice(part * width + seat * span, part * width + (seat + 1) * span)
            first.ref[seat, :, part * span : (part + 1) * span] = weights[:, columns].astype(LOW)
        first.ref[seat, :, 3 * span :] = extra


def pack_more_body(chosen, w_up, w_out, w_down, cotangent, second, down_low, own_dy):
    count, _, wide = second.ref.shape
    hidden_own = wide - w_out.ref.shape[1]
    up = w_up.get()
    out_low = w_out.get()[...].astype(LOW)
    for seat in range(count):
        columns = slice(seat * hidden_own, (seat + 1) * hidden_own)
        second.ref[seat, :, :hidden_own] = up[:, columns].astype(LOW)
        second.ref[seat, :, hidden_own:] = out_low
    second.send()
    down_low.ref[...] = w_down.get()[...].astype(LOW)
    down_low.send()
    picker = one_hot_columns(chosen.get()[...], cotangent.ref.shape[0]).astype(LOW)
    own_dy.ref[...] = mul_left_t(picker, cotangent.get()[...]).astype(LOW)


def start_pieces(pieces, into, rank, axis):
    for mask, piece in enumerate(pieces):
        place = into.at[:, rank ^ mask] if axis else into.at[rank ^ mask]
        piece.start(place)


def start_columns(columns, into, mine):
    half, routed, _ = columns[0].ref.shape
    places = into.reshape(half, 2, routed, into.shape[1])
    for mask, column in enumerate(columns):
        column.start(places.at[:, (mine & 1) ^ mask])


def start_rows(pieces, into, mine):
    routed = into.shape[0] // len(pieces)
    for mask, piece in enumerate(pieces):
        start = pl.multiple_of((mine ^ mask) * routed, routed)
        piece.start(into.at[pl.ds(start, routed), :])


def attend_body(info, lengths, *rest):
    pieces, row_pieces = rest[:4], rest[4:6]
    stream, params, joined, input_one, probs, heads, weights, sides = rest[-8:]
    count, _, shard, wide = weights.shape
    total, width = stream.ref.shape
    span = width // count
    routed = total // count
    mine, rank = info[0], info[1]
    start_pieces(pieces, weights, rank, 1)
    start_columns(row_pieces, stream.ref, mine)
    for piece in pieces:
        piece.get()
    sides[...] = weights[:, rank, :, 3 * span :]
    nat = weights[...].reshape(width, wide)
    weight_qkv = nat[:, : 3 * span]
    scale = jnp.transpose(nat[:, 3 * span :].astype(FULL))[0:8]
    params.ref[...] = scale
    params.send()
    lines = []
    for seat in range(count):
        line = sides[seat, 0:16].astype(FULL)[:, 128 - routed :]
        lines.append(line[0:1] * 256.0 + line[1:2])
    key_place = jnp.concatenate(lines, axis=1)
    query_place = jnp.transpose(jnp.broadcast_to(key_place, (8, total)))[:, 0:1]
    end = 0
    key_seg = jnp.zeros_like(key_place)
    query_seg = jnp.zeros_like(query_place)
    for part in range(lengths.shape[1]):
        end = end + lengths[0, part]
        bound = end.astype(FULL)
        key_seg = key_seg + jnp.where(key_place >= bound, 1.0, 0.0)
        query_seg = query_seg + jnp.where(query_place >= bound, 1.0, 0.0)
    allowed = (query_seg == key_seg) & (key_place <= query_place)
    for piece in row_pieces:
        piece.get()
    stream.send()
    normed, _ = normalize(stream.ref[...].astype(FULL))
    low_one = (normed * scale[0:1] + scale[1:2]).astype(LOW)
    input_one.ref[...] = low_one
    input_one.send()
    mixed = mul(low_one, weight_qkv).astype(LOW)
    joined.ref[...] = mixed
    joined.send()
    outs = []
    heads_here = probs.ref.shape[0]
    head_size = span // heads_here
    for head in range(heads_here):
        at = head * head_size
        query = mixed[:, at : at + head_size]
        key = mixed[:, span + at : span + at + head_size]
        value = mixed[:, 2 * span + at : 2 * span + at + head_size]
        raw = jnp.where(allowed, mul_right_t(query, key) * 0.125, MASKED)
        expo = jnp.exp(raw - jnp.max(raw, axis=-1, keepdims=True))
        prob = expo * (1.0 / jnp.sum(expo, axis=-1, keepdims=True))
        probs.ref[head] = prob
        outs.append(mul(prob.astype(LOW), value))
    heads.ref[...] = jnp.concatenate(outs, axis=1).astype(LOW)


def start_heads(pieces, into, mine):
    for mask, piece in enumerate(pieces):
        seat = mine ^ mask
        piece.start(into.at[seat >> 1, seat & 1])


def join_heads(blocks):
    seats = [(place, side) for place in range(blocks.shape[0]) for side in range(2)]
    return jnp.concatenate([blocks[place, side] for place, side in seats], axis=1)


def mlp_body(info, stream, params, *rest):
    second, downs = rest[:4], rest[4:8]
    sent_heads, activated, grad_hidden, grad_mlp, input_two = rest[-18:-13]
    attn_part, middle_part, own_attn, sums = rest[-13:-9]
    mlp_give, mlp_keep, logit = rest[-9:-6]
    weight_down, up_out, branch, back_rows, attended, mlp_rows = rest[-6:]
    count, total, span = sent_heads.ref.shape
    dy_pieces, head_pieces = rest[8 : 8 + count], rest[8 + count : 8 + 2 * count]
    width = span * count
    routed = total // count
    hidden_own = activated.ref.shape[1]
    mine, rank = info[0], info[1]
    start_heads(head_pieces, attended, mine)
    start_pieces(second, up_out, rank, 1)
    start_rows(dy_pieces, back_rows, mine)
    start_pieces(downs, weight_down, rank, 0)
    inputs = stream.get()[...].astype(FULL)
    for piece in head_pieces:
        piece.get()
    heads = join_heads(attended)
    for piece in second:
        piece.get()
    weight_up = up_out[:, :, :, :hidden_own].reshape(width, hidden_own)
    weight_out = up_out[:, :, :, hidden_own:].reshape(width, width)
    attn = mul(heads, weight_out)
    branch[...] = attn
    start = pl.multiple_of(mine * routed, routed)
    own_attn.ref[...] = branch[pl.ds(start, routed), :]
    own_attn.send()
    normed, inverse = normalize(inputs + attn)
    scale = params.get()[...]
    gain_two = scale[2:3]
    low_two = (normed * gain_two + scale[3:4]).astype(LOW)
    input_two.ref[...] = low_two
    input_two.send()
    act, slope = gelu_both(mul(low_two, weight_up))
    act = act.astype(LOW)
    activated.ref[...] = act
    activated.send()
    for piece in dy_pieces:
        piece.get()
    gate = gate_of(inputs, scale)
    grad_result = back_rows[...].astype(FULL)
    grad_branch = gate * grad_result
    low_mlp = grad_branch.astype(LOW)
    grad_mlp.ref[...] = low_mlp
    grad_mlp.send()
    for piece in downs:
        piece.get()
    down = rows_of(weight_down[...])
    low_hidden = (mul_right_t(low_mlp, down) * slope).astype(LOW)
    grad_hidden.ref[...] = low_hidden
    grad_hidden.send()
    part = mul_right_t(low_hidden, weight_up)
    sums.ref[...] = jnp.zeros_like(sums.ref)
    sums.ref[0:1] = jnp.sum(part * normed, axis=0, keepdims=True)
    sums.ref[1:2] = jnp.sum(part, axis=0, keepdims=True)
    middle = norm_back(normed, inverse, part * gain_two)
    middle_part.ref[...] = middle.astype(LOW)
    middle_part.send()
    seat_of = lax.broadcasted_iota(jnp.int32, (total, 1), 0) // routed
    low_attn = (middle + jnp.where(seat_of == mine, grad_branch, 0.0)).astype(LOW)
    attn_part.ref[...] = low_attn
    attn_part.send()
    back = mul_right_t(low_attn, weight_out).astype(LOW)
    for seat in range(count):
        sent_heads.ref[seat] = back[:, seat * span : (seat + 1) * span]
    sent_heads.send()
    mlp_part = mul(act, down)
    mlp_rows[...] = mlp_part.astype(LOW)
    split_rows(mlp_rows, mine, mlp_keep, mlp_give)
    logit.ref[...] = jnp.sum(grad_result * mlp_part, axis=-1, keepdims=True)
    own_dy = back_rows[pl.ds(start, routed), :].astype(FULL)
    own = jnp.sum(own_dy * branch[pl.ds(start, routed), :], axis=-1, keepdims=True)
    logit.ref[pl.ds(start, routed), :] += own
    logits = logit.ref[...] * (gate * (1.0 - gate))
    logit.ref[...] = logits
    logit.send()
    sums.ref[2:3] = jnp.sum(logits * inputs, axis=0, keepdims=True)


def split_rows(source, mine, keep, give):
    slots = keep.ref.shape[0]
    routed = source.shape[0] // (2 * slots)
    for first, into in ((1, give), (0, keep)):
        for slot in range(slots):
            start = pl.multiple_of((mine ^ (2 * slot + first)) * routed, routed)
            into.put(source.at[pl.ds(start, routed), :], slot)


def split_owner(source, rank, keep, give, axis):
    for first, into in ((1, give), (0, keep)):
        for slot in range(2):
            mask = 2 * slot + first
            into.put(source.at[:, rank ^ mask] if axis else source.at[rank ^ mask], slot)


def weight_grads_body(info, input_two, grad_hidden, attn_part, activated, grad_mlp, *rest):
    head_pieces, (give, keep, down_give, down_keep) = rest[:-7], rest[-7:-3]
    early, down, attended = rest[-3:]
    mine, rank = info[0], info[1]
    start_heads(head_pieces, attended, mine)
    hidden_own = grad_hidden.ref.shape[1]
    grad_up = mul_left_t(input_two.get()[...], grad_hidden.get()[...])
    early[:, :, :, :hidden_own] = grad_up.astype(LOW).reshape(*early.shape[:3], hidden_own)
    for piece in head_pieces:
        piece.get()
    grad_out = mul_left_t(join_heads(attended), attn_part.get()[...])
    grad_out = grad_out.astype(LOW)
    early[:, :, :, hidden_own:] = grad_out.reshape(*early.shape[:3], grad_out.shape[1])
    split_owner(early, rank, keep, give, 1)
    grad_down = mul_left_t(activated.get()[...], grad_mlp.get()[...])
    down[...] = grad_down.astype(LOW).reshape(down.shape)
    split_owner(down, rank, down_keep, down_give, 0)


def sum_blocks(blocks):
    result = blocks[0].astype(FULL)
    for seat in range(1, blocks.shape[0]):
        result = result + blocks[seat].astype(FULL)
    return result


def back_body(info, joined, probs, input_one, stream, more_sums, *rest):
    params, middle_part, logit = rest[:3]
    pieces_in, got_parts, late_parts = rest[3:7], rest[7], rest[8:12]
    give, keep, weights, late, sums, part_rows = rest[12:]
    width = stream.ref.shape[1]
    span = got_parts.ref.shape[2]
    rank = info[1]
    start_pieces(pieces_in, weights, rank, 1)
    grad = sum_blocks(got_parts.get()).astype(LOW)
    mixed = joined.get()[...]
    chances = probs.get()
    pieces = ([], [], [])
    heads_here = chances.shape[0]
    head_size = span // heads_here
    for head in range(heads_here):
        at = head * head_size
        query = mixed[:, at : at + head_size]
        key = mixed[:, span + at : span + at + head_size]
        value = mixed[:, 2 * span + at : 2 * span + at + head_size]
        grad_head = grad[:, at : at + head_size]
        prob = chances[head]
        grad_prob = mul_right_t(grad_head, value)
        delta = jnp.sum(prob * grad_prob, axis=-1, keepdims=True)
        grad_score = (prob * (grad_prob - delta)).astype(LOW)
        pieces[0].append(mul(grad_score, key) * 0.125)
        pieces[1].append(mul_left_t(grad_score, query) * 0.125)
        pieces[2].append(mul_left_t(prob.astype(LOW), grad_head))
    grad_joined = jnp.concatenate([*pieces[0], *pieces[1], *pieces[2]], axis=1).astype(LOW)
    grad_qkv = mul_left_t(input_one.get()[...], grad_joined)
    late[:, :, :, : 3 * span] = grad_qkv.astype(LOW).reshape(*late.shape[:3], 3 * span)
    for piece in pieces_in:
        piece.get()
    weight_qkv = weights[...].reshape(width, weights.shape[3])[:, : 3 * span]
    part = mul_right_t(grad_joined, weight_qkv)
    normed, inverse = normalize(stream.get()[...].astype(FULL))
    sums[...] = jnp.zeros_like(sums)
    sums[0:1] = jnp.sum(part * normed, axis=0, keepdims=True)
    sums[1:2] = jnp.sum(part, axis=0, keepdims=True)
    sums[2:5] = more_sums.get()[0:3]
    turned = jnp.transpose(sums[...]).astype(LOW)
    late[:, :, :, 3 * span :] = turned.reshape(*late.shape[:3], 128)
    for mask, late_part in enumerate(late_parts):
        late_part.put(late.at[:, rank ^ mask])
    scale = params.get()[...]
    whole = middle_part.get()[...].astype(FULL) + norm_back(normed, inverse, part * scale[0:1])
    part_rows[...] = (whole + logit.get()[...] * scale[4:5]).astype(LOW)
    split_rows(part_rows, info[0], keep, give)


def near_body(*refs):
    pairs = len(refs) // 4
    for kind in range(pairs):
        arrived = refs[2 * kind + 1].get()
        kept = refs[2 * kind].get()
        first, second = refs[2 * pairs + 2 * kind : 2 * pairs + 2 * kind + 2]
        second.ref[...] = (kept[1].astype(FULL) + arrived[1].astype(FULL)).astype(LOW)
        second.send()
        first.ref[...] = (kept[0].astype(FULL) + arrived[0].astype(FULL)).astype(first.ref.dtype)
        first.send()


def far_body(kept, far, result):
    total = kept.get()[...].astype(FULL) + far.get()[...].astype(FULL)
    result.ref[...] = total.astype(result.ref.dtype)


def sum_squares(part):
    by_column = jnp.sum(part * part, axis=0, keepdims=True)
    return jnp.sum(by_column, axis=1, keepdims=True)


def early_squares_body(early_low, early_got, down_first, down_far, squares, shard_down):
    count, _, wide = early_low.ref.shape
    part = down_first.get()[...].astype(FULL) + down_far.get()[...].astype(FULL)
    shard_down.ref[...] = part
    shard_down.send()
    hidden_own = wide - part.shape[1]
    total = sum_squares(part)
    own = early_low.get()
    for seat in range(count):
        total = total + sum_squares(own[seat, :, :hidden_own].astype(FULL))
    total = total + sum_squares(sum_blocks(early_got.get()[:, :, hidden_own:]))
    squares.ref[...] = jnp.broadcast_to(total, squares.ref.shape)


def late_body(zero, one, two, three, early_squares, late_low):
    count, shard, wide = late_low.ref.shape
    own = slice(0, wide - 128)
    total = early_squares.get()[0:1, 0:1]
    line = lax.broadcasted_iota(jnp.int32, (128, 128), 0)
    lane = lax.broadcasted_iota(jnp.int32, (128, 128), 1)
    beside = jnp.zeros((shard, 128), FULL)
    for seat in range(count):
        part = zero.get()[seat].astype(FULL)
        for other in (one, two, three):
            part = part + other.get()[seat].astype(FULL)
        part = part.astype(LOW)
        late_low.ref[seat, :, own] = part[:, own]
        total = total + sum_squares(part[:, own].astype(FULL))
        move = ((line < 8) & (lane == line + 8 * (seat + 1))).astype(FULL).astype(LOW)
        beside = beside + mul(part[:, wide - 128 :], move)
    high = total.astype(LOW).astype(FULL)
    middle = (total - high).astype(LOW).astype(FULL)
    rest = total - high - middle
    lane = lane[0:shard]
    beside = jnp.where(lane == 0, high, beside)
    beside = jnp.where(lane == 1, middle, beside)
    beside = jnp.where(lane == 2, rest, beside).astype(LOW)
    for seat in range(count):
        late_low.ref[seat, :, wide - 128 :] = beside


def norm_body(late_got, squares, sides):
    count, shard, wide = late_got.get().shape
    beside = late_got.get()[:, :, wide - 128 :].astype(FULL)
    total = beside[0]
    for seat in range(1, count):
        total = total + beside[seat]
    sides.ref[...] = total
    line = lax.broadcasted_iota(jnp.int32, total.shape, 0)
    lane = lax.broadcasted_iota(jnp.int32, total.shape, 1)
    terms = jnp.where((line == 0) & (lane < 3), total, 0.0)
    vectors = jnp.where(lane >= 8, total * total, 0.0)
    result = jnp.sum(jnp.sum(terms + vectors, axis=0, keepdims=True), axis=1, keepdims=True)
    squares.ref[...] = jnp.broadcast_to(result, squares.ref.shape)


def neighbour_body(keep, near, *blocks):
    arrived = near.get()
    kept = keep.get()
    for slot, block in enumerate(blocks):
        block.ref[...] = (kept[slot].astype(FULL) + arrived[slot].astype(FULL)).astype(LOW)
        block.send()


def put_rows(picker, stream, rows):
    placed = mul(picker.astype(LOW), rows.astype(LOW)).astype(LOW)
    taken = jnp.sum(picker, axis=-1, keepdims=True) > 0.0
    return jnp.where(taken, placed.astype(FULL), stream.astype(FULL)).astype(LOW)


def mixed_body(chosen, tokens, params, own_x, own_attn, *rest):
    *parts, mixed = rest
    inputs = own_x.get()[...].astype(FULL)
    branch = own_attn.get()[...]
    for part in parts:
        branch = branch + part.get()[...].astype(FULL)
    result = inputs + gate_of(inputs, params.get()[...]) * branch
    picker = one_hot_columns(chosen.get()[...], mixed.ref.shape[0])
    mixed.ref[...] = put_rows(picker, tokens.get()[...], result)


def grad_tokens_body(chosen, cotangent, own_dy, *rest):
    *parts, grad_tokens = rest
    result = own_dy.get()[...].astype(FULL)
    for part in parts:
        result = result + part.get()[...].astype(FULL)
    picker = one_hot_columns(chosen.get()[...], grad_tokens.ref.shape[0])
    grad_tokens.ref[...] = put_rows(picker, cotangent.get()[...], result)


def side_by_side(blocks, columns):
    return jnp.concatenate([blocks[seat, :, columns] for seat in range(blocks.shape[0])], axis=1)


def adam_body(info, squares, late_got, early_got, sides, shard_down, *rest):
    states, outs, turn = rest[:15], rest[15:-1], rest[-1]
    norm = jnp.sqrt(squares.get()[0:1, 0:1])
    outs[15].ref[...] = norm
    factor = CLIP_NORM / jnp.maximum(norm, CLIP_NORM)
    late, early = late_got.get(), early_got.get()
    count, _, wide = late.shape
    span = (wide - 128) // 3
    hidden_own = early.shape[2] - count * span
    thirds = [slice(part * span, (part + 1) * span) for part in range(3)]
    for kind in range(5):
        if kind == 0:
            grad = jnp.concatenate([side_by_side(late, third) for third in thirds], axis=1)
            grad = grad.astype(FULL)
        elif kind == 1:
            grad = sum_blocks(early[:, :, hidden_own:])
        elif kind == 2:
            grad = side_by_side(early, slice(0, hidden_own)).astype(FULL)
        elif kind == 3:
            grad = shard_down.get()[...]
        else:
            shard = sides.get().shape[0]
            turn[0:shard] = sides.get()[...]
            turn[...] = jnp.transpose(turn[...])
            start = pl.multiple_of(8 * (info[0] + 1), 8)
            grad = turn[pl.ds(start, 8), :][0:5, 0:shard]
        weight, first, second = (states[3 * kind + i].get()[...] for i in range(3))
        updated = adam_step(weight, first, second, grad, factor, RATES[kind])
        for i in range(3):
            outs[3 * kind + i].ref[...] = updated[i]
            outs[3 * kind + i].send()


def swap(values, axis, mask):
    pairs = [(index, index ^ mask) for index in range(lax.axis_size(axis))]
    return lax.ppermute(values, axis, pairs)


def exchange(blocks):
    return lax.all_to_all(blocks, "seq", 0, 0)


def share_fsdp(own, before=()):
    far = swap(own, "fsdp", 2)
    near = swap(own, "fsdp", 1)
    return own, near, far, swap(after(far, *before), "fsdp", 1)


def after(value, *others):
    return lax.optimization_barrier((value, *others))[0]


def gather_column(copies):
    count = lax.axis_size("seq")
    groups = [list(range(start, count, 2)) for start in range(2)]
    return lax.all_to_all(copies, "seq", 0, 0, axis_index_groups=groups)


def share_column(own):
    return [own] + [swap(own, "seq", mask) for mask in range(2, lax.axis_size("seq"), 2)]


def share_rows(column):
    other = [swap(block, "seq", 1) for block in column]
    return [block for pair in zip(column, other) for block in pair]


def start_reduce(pairs):
    near = [Near(swap(give, "fsdp", 1)) for give, _ in pairs]
    ins = [array for (_, keep), arrived in zip(pairs, near) for array in (keep, arrived)]
    kinds = [(keep.shape[1:], dtype) for (_, keep), dtype in zip(pairs, (LOW, FULL))]
    outs = [struct(shape, kind) for shape, dtype in kinds for kind in (dtype, LOW)]
    return local_call(near_body, outs, (), ins)


def end_reduce(first, second, wait=()):
    far = Near(swap(second, "fsdp", 2))
    out = struct(first.shape, first.dtype)
    return local_call(far_body, [out], (), [first, far], wait=wait)[0]


def start_rows_sum(near, keep, wait=()):
    outs = [struct(keep.shape[1:], LOW)] * keep.shape[0]
    return local_call(neighbour_body, outs, (), [keep, Near(near)], wait=wait)


def end_rows_sum(blocks):
    arrived = [swap(block, "seq", 2 * slot) for slot, block in enumerate(blocks) if slot]
    return [blocks[0], *map(Near, arrived)]


def sum_over(value, axes):
    for axis in axes:
        step = 1
        while step < lax.axis_size(axis):
            value = value + swap(value, axis, step)
            step *= 2
    return value


def body_split(
    tokens,
    cotangent,
    chosen,
    positions,
    lengths,
    w_qkv,
    m_qkv,
    v_qkv,
    w_out,
    m_out,
    v_out,
    w_up,
    m_up,
    v_up,
    w_down,
    m_down,
    v_down,
    vectors,
    m_vec,
    v_vec,
):
    count = lax.axis_size("seq")
    group = lax.axis_size("fsdp")
    info = jnp.stack([lax.axis_index("seq"), lax.axis_index("fsdp")]).astype(jnp.int32)
    width = tokens.shape[2]
    heads = HEADS // count
    span = width // count
    hidden_own = w_up.shape[1] // count
    shard = w_qkv.shape[0]
    piece = w_down.shape[0]
    routed = chosen.shape[1]
    total = routed * count
    wide = 3 * span + 128
    stream_low = struct((total, width), LOW)
    half_rows = struct((count // 2, routed, width), LOW)
    hidden_low = struct((total, hidden_own), LOW)
    row_sums = struct((8, width), FULL)
    stage = pltpu.VMEM((total, width), LOW)
    stage_full = pltpu.VMEM((total, width), FULL)
    stage_heads = pltpu.VMEM((count // 2, 2, total, span), LOW)
    stage_down = pltpu.VMEM((group, piece, width), LOW)
    stage_weights = pltpu.VMEM((count, group, shard, wide), LOW)

    def raw(arrays):
        return [Raw(array) for array in arrays]

    own_x, copies_x = local_call(
        pack_rows_body, [struct((routed, width), LOW), half_rows], (), [chosen, tokens[0]]
    )
    x_column = gather_column(copies_x)
    x_pieces = (x_column, swap(x_column, "seq", 1))
    (first,) = local_call(
        pack_first_body,
        [struct((count, shard, wide), LOW)],
        (),
        [chosen, positions, w_qkv, vectors.T],
        scratch=[pltpu.VMEM((shard, 128), FULL), pltpu.VMEM((128, 128), FULL)],
        wait=[Raw(own_x)],
    )
    got_first = exchange(after(first, x_column))
    second, down_low, own_dy = local_call(
        pack_more_body,
        [
            struct((count, shard, hidden_own + width), LOW),
            struct(w_down.shape, LOW),
            struct((routed, width), LOW),
        ],
        (),
        [chosen, w_up, w_out, w_down, cotangent[0]],
        wait=[Raw(first)],
    )
    down_pieces = share_fsdp(down_low)
    first_pieces = share_fsdp(got_first)
    dy_columns = share_column(after(own_dy, x_column))
    before = (x_pieces[1], *down_pieces[1:], *dy_columns[1:])
    got_second = exchange(after(second, got_first, *before))

    stream, params, joined, input_one, probs, sent_heads = local_call(
        attend_body,
        [
            stream_low,
            row_sums,
            struct((total, 3 * span), LOW),
            stream_low,
            struct((heads, total, total), FULL),
            struct((total, span), LOW),
        ],
        (info, lengths),
        raw([*first_pieces, *x_pieces]),
        scratch=[stage_weights, pltpu.VMEM((count, shard, 128), LOW)],
        spare=12,
        wait=down_pieces,
    )
    dy_pieces = share_rows([after(block, x_pieces[1]) for block in dy_columns])
    head_columns = share_column(sent_heads)
    head_pieces = share_rows(head_columns)
    got_second = after(got_second, sent_heads, *dy_pieces[1::2])
    second_pieces = share_fsdp(got_second, (*head_pieces[1::2], *dy_pieces[1::2]))
    (
        sent_heads,
        activated,
        grad_hidden,
        grad_mlp,
        input_two,
        attn_part,
        middle_part,
        own_attn,
        sums,
        mlp_give,
        mlp_keep,
        logit,
    ) = local_call(
        mlp_body,
        [
            struct((count, total, span), LOW),
            hidden_low,
            hidden_low,
            stream_low,
            stream_low,
            stream_low,
            stream_low,
            struct((routed, width), FULL),
            row_sums,
            Sink(half_rows, count // 2),
            Sink(half_rows, count // 2),
            struct((total, 1), FULL),
        ],
        (info,),
        [stream, params, *raw([*second_pieces, *down_pieces, *dy_pieces, *head_pieces])],
        scratch=[
            stage_down,
            pltpu.VMEM((count, group, shard, hidden_own + width), LOW),
            stage_full,
            stage,
            stage_heads,
            stage,
        ],
        spare=18,
    )
    got_parts = exchange(sent_heads)
    early_pair = struct((2, count, shard, hidden_own + width), LOW)
    down_pair = struct((2, piece, width), LOW)
    early_give, early_keep, down_give, down_keep = local_call(
        weight_grads_body,
        [Sink(early_pair, 2), Sink(early_pair, 2), Sink(down_pair, 2), Sink(down_pair, 2)],
        (info,),
        [input_two, grad_hidden, attn_part, activated, grad_mlp, *raw(head_pieces)],
        scratch=[
            pltpu.VMEM((count, group, shard, hidden_own + width), LOW),
            stage_down,
            stage_heads,
        ],
        spare=10,
    )
    early_first, early_second, down_first, down_second = start_reduce(
        [(early_give, early_keep), (down_give, down_keep)]
    )
    mlp_near = swap(mlp_give, "seq", 1)
    early_low = end_reduce(early_first, early_second, [mlp_near])
    mlp_blocks = start_rows_sum(mlp_near, mlp_keep, [Raw(early_low)])
    mlp_parts = end_rows_sum(mlp_blocks)
    late_block = struct((count, shard, wide), LOW)
    *late_parts, input_give, input_keep = local_call(
        back_body,
        [*[Sink(late_block, 1)] * 4, *[Sink(half_rows, count // 2)] * 2],
        (info,),
        [
            *(joined, probs, input_one, stream, sums),
            *(params, middle_part, logit),
            *raw(first_pieces),
            Near(got_parts),
        ],
        scratch=[
            stage_weights,
            stage_weights,
            pltpu.VMEM((128, width), FULL),
            stage,
        ],
        wait=[Raw(early_low), Raw(mlp_blocks[0])],
        spare=14,
    )
    early_got = exchange(early_low)
    late_arrived = [Near(swap(late_parts[mask], "fsdp", mask)) for mask in (1, 2, 3)]
    late_near = late_arrived[0].array
    down_far = Near(swap(after(down_second, late_near), "fsdp", 2))
    input_blocks = start_rows_sum(swap(after(input_give, late_near), "seq", 1), input_keep)
    input_parts = end_rows_sum(input_blocks)
    early_squares, shard_down = local_call(
        early_squares_body,
        [struct((8, 128), FULL), struct((piece, width), FULL)],
        (),
        [early_low, Near(early_got), down_first, down_far],
    )
    (late_low,) = local_call(
        late_body,
        [late_block],
        (),
        [late_parts[0], *late_arrived, early_squares],
        wait=[part.array for part in mlp_parts[1:]],
    )
    late_got = exchange(late_low)
    whole = struct(tokens.shape[1:], LOW)
    (mixed,) = local_call(
        mixed_body, [whole], (), [chosen, tokens[0], params, own_x, own_attn, *mlp_parts]
    )
    squares, sides = local_call(
        norm_body,
        [struct((8, 128), FULL), struct((shard, 128), FULL)],
        (),
        [Near(late_got)],
        wait=[Raw(input_blocks[0]), Raw(mixed)],
    )
    squares = sum_over(squares, ("fsdp",))
    states = (
        *(w_qkv, m_qkv, v_qkv),
        *(w_out, m_out, v_out),
        *(w_up, m_up, v_up),
        *(w_down, m_down, v_down),
        *(vectors.T, m_vec.T, v_vec.T),
    )
    *updates, grad_norm = local_call(
        adam_body,
        [*(struct(state.shape, FULL) for state in states), struct((1, 1), FULL)],
        (info,),
        [Near(squares), Near(late_got), Near(early_got), sides, shard_down, *states],
        scratch=[pltpu.VMEM((128, 128), FULL)],
    )
    (grad_tokens,) = local_call(
        grad_tokens_body,
        [whole],
        (),
        [chosen, cotangent[0], own_dy, *input_parts],
        wait=[Raw(grad_norm)],
    )
    updates = updates[:12] + [update.T for update in updates[12:]]
    return (mixed[None], grad_tokens[None], *updates, grad_norm[0, 0])


def fits_split(mesh, *arrays):
    tokens, _, chosen, positions, _, w_qkv = arrays[:6]
    w_up, w_down = arrays[11], arrays[14]
    count, group = mesh.shape["seq"], mesh.shape["fsdp"]
    width = tokens.shape[2]
    routed = chosen.shape[1] // count
    hidden = w_up.shape[1]
    return (
        group == 4
        and 1 < count <= 8
        and count & (count - 1) == 0
        and HEADS % count == 0
        and width % (count * 128) == 0
        and hidden % (count * 128) == 0
        and w_down.shape[0] == hidden
        and w_qkv.shape[0] % (count * group * 16) == 0
        and w_qkv.shape[0] // (count * group) <= 128
        and w_qkv.shape[0] == width
        and routed % 16 == 0
        and routed <= 64
        and positions.shape[1] <= 65536
    )


def solution(mesh):
    streams = (P("fsdp", "seq", None),) * 2
    states = (P(("seq", "fsdp"), None),) * 15
    placed = streams + (P("fsdp", "seq"),) * 2 + (P("fsdp", None),) + states

    def run(*arrays):
        return jax.shard_map(
            body_split if fits_split(mesh, *arrays) else body_general,
            mesh=mesh,
            in_specs=placed,
            out_specs=streams + states + (P(),),
            check_vma=False,
        )(*arrays)

    return run
```

profile of v0, /device:TPU:0, one launch (start us, length us, event | category | flops | bytes accessed | tf_op | source)
XLA Modules:
  0.0 229.4 jit_solution(15045569591522796866)
XLA Ops:
  3.1 6.3 %all-to-all-start = ((bf16[4,64,1024]{2,1,0:T(8,128)(2,1)}), bf16[4,64,1024]{2,1,0:T(8,128)(2,1)S(1)}, u32[]{:S(2)}, u32[]{:S(2)}) async-start(bf16[4,64,1024]{2,1,0:T(8,128)(2,1)} %get-tuple-element.95), calls=%async_computation | async-start | bytes 1048576 | tf_op jit(solution)/shard_map/all_to_all | solution.py:1018
  15.5 8.4 %all-to-all-done.refs_6_ = bf16[4,64,1024]{2,1,0:T(8,128)(2,1)S(1)} async-done(((bf16[4,64,1024]{2,1,0:T(8,128)(2,1)}), bf16[4,64,1024]{2,1,0:T(8,128)(2,1)S(1)}, u32[]{:S(2)}, u32[]{:S(2)}) %all-to-all-start) | async-done | bytes 524320 | tf_op jit(solution)/shard_map/all_to_all | solution.py:1018
  25.4 3.4 %all-to-all-start.1 = ((bf16[8,32,512]{2,1,0:T(8,128)(2,1)}), bf16[8,32,512]{2,1,0:T(8,128)(2,1)S(1)}, u32[]{:S(2)}, u32[]{:S(2)}) async-start(bf16[8,32,512]{2,1,0:T(8,128)(2,1)} %shard_map.332.refs_5_), calls=%async_computation.1 | async-start | bytes 524288 | tf_op jit(solution)/shard_map/all_to_all | solution.py:1002
  29.4 3.7 %collective-permute-start.9 = (bf16[64,1024]{1,0:T(8,128)(2,1)}, bf16[64,1024]{1,0:T(8,128)(2,1)S(1)}, u32[]{:S(2)}, u32[]{:S(2)}) collective-permute-start(bf16[64,1024]{1,0:T(8,128)(2,1)} %get-tuple-element.105.refs_11_.refs_2_), channel_id=1, source_target_pairs={{0,24},{4,28},{8,16},{12,20},{16,8},{20,12},{24,0},{28,4},{1,25},{... | collective-permute-start | bytes 393224 | tf_op jit(solution)/shard_map/ppermute | solution.py:998
  33.8 7.6 %collective-permute-done.9.refs_17_ = bf16[64,1024]{1,0:T(8,128)(2,1)S(1)} collective-permute-done((bf16[64,1024]{1,0:T(8,128)(2,1)}, bf16[64,1024]{1,0:T(8,128)(2,1)S(1)}, u32[]{:S(2)}, u32[]{:S(2)}) %collective-permute-start.9) | collective-permute-done | bytes 131104 | tf_op jit(solution)/shard_map/ppermute | solution.py:998
  41.4 6.9 %collective-permute-done.8.refs_15_ = bf16[64,1024]{1,0:T(8,128)(2,1)S(1)} collective-permute-done((bf16[64,1024]{1,0:T(8,128)(2,1)}, bf16[64,1024]{1,0:T(8,128)(2,1)S(1)}, u32[]{:S(2)}, u32[]{:S(2)}) %collective-permute-start.8) | collective-permute-done | bytes 131104 | tf_op jit(solution)/shard_map/ppermute | solution.py:998
  49.2 3.5 %all-to-all-start.2 = ((bf16[8,32,1536]{2,1,0:T(8,128)(2,1)}), bf16[8,32,1536]{2,1,0:T(8,128)(2,1)S(1)}, u32[]{:S(2)}, u32[]{:S(2)}) async-start(bf16[8,32,1536]{2,1,0:T(8,128)(2,1)} %get-tuple-element.103), calls=%async_computation.2 | async-start | bytes 1572864 | tf_op jit(solution)/shard_map/all_to_all | solution.py:1002
  54.3 5.5 %collective-permute-done.1.refs_4_.refs_11_ = bf16[8,32,512]{2,1,0:T(8,128)(2,1)S(1)} collective-permute-done((bf16[8,32,512]{2,1,0:T(8,128)(2,1)S(1)}, bf16[8,32,512]{2,1,0:T(8,128)(2,1)S(1)}, u32[]{:S(2)}, u32[]{:S(2)}) %collective-permute-start.1) | collective-permute-done | bytes 262176 | tf_op jit(solution)/shard_map/ppermute | solution.py:998
  65.1 6.0 %shard_map.334 = (bf16[512,1024]{1,0:T(8,128)(2,1)}, f32[8,1024]{1,0:T(8,128)}, bf16[512,384]{1,0:T(8,128)(2,1)}, bf16[512,1024]{1,0:T(8,128)(2,1)}, f32[2,512,512]{2,1,0:T(8,128)}, /*index=5*/bf16[512,128]{1,0:T(8,128)(2,1)}) custom-call(s32[2]{0:T(128)S(1)} %pad_add_fusion.refs_0_, s32[1,3]{1,0:T(1,128)S(1)} %copy-done.4, bf16[8,32,512]{2,1,0:T(8,128)(2,1)} %copy-done.6, ...), custom_call_target="tpu_custom_call" | custom-call | flops 1024 | bytes 1024 | tf_op jit(solution)/shard_map/pallas_call | solution.py:484
  87.0 6.1 %collective-permute-done.19.refs_23_.refs_10_ = bf16[512,128]{1,0:T(8,128)(2,1)S(1)} collective-permute-done((bf16[512,128]{1,0:T(8,128)(2,1)}, bf16[512,128]{1,0:T(8,128)(2,1)S(1)}, u32[]{:S(2)}, u32[]{:S(2)}) %collective-permute-start.19) | collective-permute-done | bytes 131104 | tf_op jit(solution)/shard_map/ppermute | solution.py:998
  95.2 4.3 %collective-permute-done.20.refs_24_.refs_11_ = bf16[512,128]{1,0:T(8,128)(2,1)S(1)} collective-permute-done((bf16[512,128]{1,0:T(8,128)(2,1)S(1)}, bf16[512,128]{1,0:T(8,128)(2,1)S(1)}, u32[]{:S(2)}, u32[]{:S(2)}) %collective-permute-start.20) | collective-permute-done | bytes 131104 | tf_op jit(solution)/shard_map/ppermute | solution.py:998
  104.6 12.8 %shard_map.335 = (bf16[8,512,128]{2,1,0:T(8,128)(2,1)}, bf16[512,512]{1,0:T(8,128)(2,1)}, bf16[512,512]{1,0:T(8,128)(2,1)}, bf16[512,1024]{1,0:T(8,128)(2,1)}, b...) custom-call(s32[2]{0:T(128)S(1)} %pad_add_fusion.refs_0_, ...), custom_call_target="tpu_custom_call" | custom-call | flops 1024 | bytes 1024 | tf_op jit(solution)/shard_map/pallas_call | solution.py:484
  117.4 6.7 %shard_map.336 = (bf16[2,8,32,1536]{3,2,1,0:T(8,128)(2,1)}, bf16[2,8,32,1536]{3,2,1,0:T(8,128)(2,1)}, bf16[2,128,1024]{2,1,0:T(8,128)(2,1)}, bf16[2,128,1024]{2,1,0:T(8,128)(2,1)}) custom-call(s32[2]{0:T(128)S(1)} %pad_add_fusion.refs_0_, bf16[512,1024]{1,0:T(8,128)(2,1)} %get-tuple-element.114.refs_1_, bf16[512,512]{1,0:T(8,128)(2,1)} %get-tuple-element.115.refs_2_, ...), custom_call_target="tpu_custom_call" | custom-call | flops 1024 | bytes 1024 | tf_op jit(solution)/shard_map/pallas_call | solution.py:484
  124.4 3.6 %all-to-all-start.3 = ((bf16[8,512,128]{2,1,0:T(8,128)(2,1)}), bf16[8,512,128]{2,1,0:T(8,128)(2,1)S(1)}, u32[]{:S(2)}, u32[]{:S(2)}) async-start(bf16[8,512,128]{2,1,0:T(8,128)(2,1)} %get-tuple-element.135), calls=%async_computation.3 | async-start | bytes 2097152 | tf_op jit(solution)/shard_map/all_to_all | solution.py:1002
  129.9 3.2 %shard_map.337 = (bf16[8,32,1536]{2,1,0:T(8,128)(2,1)}, bf16[8,32,1536]{2,1,0:T(8,128)(2,1)}, f32[128,1024]{1,0:T(8,128)}, bf16[128,1024]{1,0:T(8,128)(2,1)}) custom-call(bf16[2,8,32,1536]{3,2,1,0:T(8,128)(2,1)} %get-tuple-element.119.refs_0_, bf16[2,8,32,1536]{3,2,1,0:T(8,128)(2,1)S(1)} %collective-permute-done.25.refs_1_, ...), custom_call_target="tpu_custom_call" | custom-call | flops 1024 | bytes 1024 | tf_op jit(solution)/shard_map/pallas_call | solution.py:484
  135.5 18.8 %collective-permute-done.24.refs_2_.refs_1_ = bf16[4,64,1024]{2,1,0:T(8,128)(2,1)S(1)} collective-permute-done((bf16[4,64,1024]{2,1,0:T(8,128)(2,1)S(1)}, bf16[4,64,1024]{2,1,0:T(8,128)(2,1)S(1)}, u32[]{:S(2)}, u32[]{:S(2)}) %collective-permute-start.24) | collective-permute-done | bytes 524320 | tf_op jit(solution)/shard_map/ppermute | solution.py:998
  156.7 5.9 %all-to-all-start.4 = ((bf16[8,32,1536]{2,1,0:T(8,128)(2,1)}), bf16[8,32,1536]{2,1,0:T(8,128)(2,1)S(1)}, u32[]{:S(2)}, u32[]{:S(2)}) async-start(bf16[8,32,1536]{2,1,0:T(8,128)(2,1)} %shard_map.338.refs_2_.refs_14_.refs_0_), calls=%async_computation.4 | async-start | bytes 1572864 | tf_op jit(solution)/shard_map/all_to_all | solution.py:1002
  164.6 8.9 %shard_map.341 = (bf16[8,32,512]{2,1,0:T(8,128)(2,1)}, bf16[8,32,512]{2,1,0:T(8,128)(2,1)}, bf16[8,32,512]{2,1,0:T(8,128)(2,1)}, bf16[8,32,512]{2,1,0:T(8,128)(2...) custom-call(s32[2]{0:T(128)S(1)} %pad_add_fusion.refs_0_, bf16[512,384]{1,0:T(8,128)(2,1)} %get-tuple-element.129.refs_1_, ...), custom_call_target="tpu_custom_call" | custom-call | flops 1024 | bytes 1024 | tf_op jit(solution)/shard_map/pallas_call | solution.py:484
  180.8 3.9 %collective-permute-done.28.refs_6_.refs_5_ = bf16[64,1024]{1,0:T(8,128)(2,1)S(1)} collective-permute-done((bf16[64,1024]{1,0:T(8,128)(2,1)S(1)}, bf16[64,1024]{1,0:T(8,128)(2,1)S(1)}, u32[]{:S(2)}, u32[]{:S(2)}) %collective-permute-start.28) | collective-permute-done | bytes 131104 | tf_op jit(solution)/shard_map/ppermute | solution.py:998
  184.7 3.6 %collective-permute-start.30 = (bf16[64,1024]{1,0:T(8,128)(2,1)S(1)}, bf16[64,1024]{1,0:T(8,128)(2,1)S(1)}, u32[]{:S(2)}, u32[]{:S(2)}) collective-permute-start(bf16[64,1024]{1,0:T(8,128)(2,1)S(1)} %copy-done.29), channel_id=1, source_target_pairs={{0,24},{4,28},{8,16},{12,20},{16,8},{20,12},{24,0},{28,4},{1,25},{... | collective-permute-start | bytes 393224 | tf_op jit(solution)/shard_map/ppermute | solution.py:998
  190.6 5.3 %collective-permute-done.29.refs_7_.refs_6_ = bf16[64,1024]{1,0:T(8,128)(2,1)S(1)} collective-permute-done((bf16[64,1024]{1,0:T(8,128)(2,1)S(1)}, bf16[64,1024]{1,0:T(8,128)(2,1)S(1)}, u32[]{:S(2)}, u32[]{:S(2)}) %collective-permute-start.29) | collective-permute-done | bytes 131104 | tf_op jit(solution)/shard_map/ppermute | solution.py:998
  198.0 5.9 %all-to-all-start.5 = ((bf16[8,32,512]{2,1,0:T(8,128)(2,1)}), bf16[8,32,512]{2,1,0:T(8,128)(2,1)S(1)}, u32[]{:S(2)}, u32[]{:S(2)}) async-start(bf16[8,32,512]{2,1,0:T(8,128)(2,1)} %shard_map.344), calls=%async_computation.5 | async-start | bytes 524288 | tf_op jit(solution)/shard_map/all_to_all | solution.py:1002
  220.4 5.2 %shard_map.346 = (f32[32,3072]{1,0:T(8,128)}, f32[32,3072]{1,0:T(8,128)}, f32[32,3072]{1,0:T(8,128)}, f32[32,1024]{1,0:T(8,128)}, f32[32,1024]{1,0:T(8,128)}, /*...) custom-call(s32[2]{0:T(128)S(1)} %pad_add_fusion.refs_0_, ...), custom_call_target="tpu_custom_call" | custom-call | flops 1024 | bytes 1024 | tf_op jit(solution)/shard_map/pallas_call | solution.py:484
  225.7 3.5 %shard_map.347 = bf16[512,1024]{1,0:T(8,128)(2,1)} custom-call(s32[1,64]{1,0:T(1,128)} %refs_0_.9, bf16[512,1024]{1,0:T(8,128)(2,1)} %bitcast.16, bf16[64,1024]{1,0:T(8,128)(2,1)} %get-tuple-element.105.refs_11_.refs_2_, bf16[64,1024]{1,0:T(8,128)(2,1)} %get-tuple-element.140.refs_1_.refs_3_, bf16[64,1024]{1,0:T(8,128)(2,1)S(1)} %collective-permute-done.33.refs_4_, ...), custom_call_target="tpu_custom_call" | custom-call | flops 1024 | bytes 1024 | tf_op jit(solution)/shard_map/pallas_call | solution.py:484
  (154 shorter events, 79.1 us)
Async XLA Ops:
  3.1 20.8 %all-to-all-start = ((bf16[4,64,1024]{2,1,0:T(8,128)(2,1)}), bf16[4,64,1024]{2,1,0:T(8,128)(2,1)S(1)}, u32[]{:S(2)}, u32[]{:S(2)}) async-start(bf16[4,64,1024]{2,1,0:T(8,128)(2,1)} %get-tuple-element.95), calls=%async_computation | async-start | bytes 1048576 | tf_op jit(solution)/shard_map/all_to_all | solution.py:1018
  13.9 15.0 %collective-permute-start.5 = (bf16[128,1024]{1,0:T(8,128)(2,1)}, bf16[128,1024]{1,0:T(8,128)(2,1)S(1)}, u32[]{:S(2)}, u32[]{:S(2)}) collective-permute-start(bf16[128,1024]{1,0:T(8,128)(2,1)} %get-tuple-element.97.refs_8_.refs_7_), channel_id=1, source_target_pairs={{0,2},{1,3},{2,0},{3,1},{4,6},{5,7},{6,4},{7,5},{8,10},{9,11},{10,... | collective-permute-start | bytes 786440 | tf_op jit(solution)/shard_map/ppermute | solution.py:998
  23.9 24.4 %collective-permute-start.3 = (bf16[4,64,1024]{2,1,0:T(8,128)(2,1)S(1)}, bf16[4,64,1024]{2,1,0:T(8,128)(2,1)S(1)}, u32[]{:S(2)}, u32[]{:S(2)}) collective-permute-start(bf16[4,64,1024]{2,1,0:T(8,128)(2,1)S(1)} %all-to-all-done.refs_6_), channel_id=1, source_target_pairs={{0,4},{4,0},{8,12},{12,8},{16,20},{20,16},{24,28},{28,24},{1,5},{5... | collective-permute-start | bytes 1572872 | tf_op jit(solution)/shard_map/ppermute | solution.py:998
  25.4 22.9 %all-to-all-start.1 = ((bf16[8,32,512]{2,1,0:T(8,128)(2,1)}), bf16[8,32,512]{2,1,0:T(8,128)(2,1)S(1)}, u32[]{:S(2)}, u32[]{:S(2)}) async-start(bf16[8,32,512]{2,1,0:T(8,128)(2,1)} %shard_map.332.refs_5_), calls=%async_computation.1 | async-start | bytes 524288 | tf_op jit(solution)/shard_map/all_to_all | solution.py:1002
  29.4 12.0 %collective-permute-start.9 = (bf16[64,1024]{1,0:T(8,128)(2,1)}, bf16[64,1024]{1,0:T(8,128)(2,1)S(1)}, u32[]{:S(2)}, u32[]{:S(2)}) collective-permute-start(bf16[64,1024]{1,0:T(8,128)(2,1)} %get-tuple-element.105.refs_11_.refs_2_), channel_id=1, source_target_pairs={{0,24},{4,28},{8,16},{12,20},{16,8},{20,12},{24,0},{28,4},{1,25},{... | collective-permute-start | bytes 393224 | tf_op jit(solution)/shard_map/ppermute | solution.py:998
  33.1 15.2 %collective-permute-start.8 = (bf16[64,1024]{1,0:T(8,128)(2,1)}, bf16[64,1024]{1,0:T(8,128)(2,1)S(1)}, u32[]{:S(2)}, u32[]{:S(2)}) collective-permute-start(bf16[64,1024]{1,0:T(8,128)(2,1)} %get-tuple-element.105.refs_11_.refs_2_), channel_id=1, source_target_pairs={{0,16},{4,20},{8,24},{12,28},{16,0},{20,4},{24,8},{28,12},{1,17},{... | collective-permute-start | bytes 393224 | tf_op jit(solution)/shard_map/ppermute | solution.py:998
  33.1 15.2 %collective-permute-start.7 = (bf16[64,1024]{1,0:T(8,128)(2,1)}, bf16[64,1024]{1,0:T(8,128)(2,1)S(1)}, u32[]{:S(2)}, u32[]{:S(2)}) collective-permute-start(bf16[64,1024]{1,0:T(8,128)(2,1)} %get-tuple-element.105.refs_11_.refs_2_), channel_id=1, source_target_pairs={{0,8},{4,12},{8,0},{12,4},{16,24},{20,28},{24,16},{28,20},{1,9},{5... | collective-permute-start | bytes 393224 | tf_op jit(solution)/shard_map/ppermute | solution.py:998
  49.2 27.2 %all-to-all-start.2 = ((bf16[8,32,1536]{2,1,0:T(8,128)(2,1)}), bf16[8,32,1536]{2,1,0:T(8,128)(2,1)S(1)}, u32[]{:S(2)}, u32[]{:S(2)}) async-start(bf16[8,32,1536]{2,1,0:T(8,128)(2,1)} %get-tuple-element.103), calls=%async_computation.2 | async-start | bytes 1572864 | tf_op jit(solution)/shard_map/all_to_all | solution.py:1002
  61.9 12.1 %collective-permute-start.12 = (bf16[64,1024]{1,0:T(8,128)(2,1)}, bf16[64,1024]{1,0:T(8,128)(2,1)}, u32[]{:S(2)}, u32[]{:S(2)}) collective-permute-start(bf16[64,1024]{1,0:T(8,128)(2,1)} %copy-done.24), channel_id=1, source_target_pairs={{0,4},{4,0},{8,12},{12,8},{16,20},{20,16},{24,28},{28,24},{1,5},{5... | collective-permute-start | bytes 393224 | tf_op jit(solution)/shard_map/ppermute | solution.py:998
  63.6 12.7 %collective-permute-start.11 = (bf16[64,1024]{1,0:T(8,128)(2,1)}, bf16[64,1024]{1,0:T(8,128)(2,1)}, u32[]{:S(2)}, u32[]{:S(2)}) collective-permute-start(bf16[64,1024]{1,0:T(8,128)(2,1)} %copy-done.25), channel_id=1, source_target_pairs={{0,4},{4,0},{8,12},{12,8},{16,20},{20,16},{24,28},{28,24},{1,5},{5... | collective-permute-start | bytes 393224 | tf_op jit(solution)/shard_map/ppermute | solution.py:998
  76.4 25.0 %collective-permute-start.15 = (bf16[8,32,1536]{2,1,0:T(8,128)(2,1)S(1)}, bf16[8,32,1536]{2,1,0:T(8,128)(2,1)S(1)}, u32[]{:S(2)}, u32[]{:S(2)}) collective-permute-start(bf16[8,32,1536]{2,1,0:T(8,128)(2,1)S(1)} %all-to-all-done.2.refs_3_), channel_id=1, source_target_pairs={{0,2},{1,3},{2,0},{3,1},{4,6},{5,7},{6,4},{7,5},{8,10},{9,11},{10,... | collective-permute-start | bytes 2359304 | tf_op jit(solution)/shard_map/ppermute | solution.py:998
  81.0 12.1 %collective-permute-start.19 = (bf16[512,128]{1,0:T(8,128)(2,1)}, bf16[512,128]{1,0:T(8,128)(2,1)S(1)}, u32[]{:S(2)}, u32[]{:S(2)}) collective-permute-start(bf16[512,128]{1,0:T(8,128)(2,1)} %get-tuple-element.104.refs_19_.refs_6_), channel_id=1, source_target_pairs={{0,16},{4,20},{8,24},{12,28},{16,0},{20,4},{24,8},{28,12},{1,17},{... | collective-permute-start | bytes 393224 | tf_op jit(solution)/shard_map/ppermute | solution.py:998
  82.3 12.9 %collective-permute-start.16 = (bf16[512,128]{1,0:T(8,128)(2,1)}, bf16[512,128]{1,0:T(8,128)(2,1)S(1)}, u32[]{:S(2)}, u32[]{:S(2)}) collective-permute-start(bf16[512,128]{1,0:T(8,128)(2,1)} %get-tuple-element.104.refs_19_.refs_6_), channel_id=1, source_target_pairs={{0,4},{4,0},{8,12},{12,8},{16,20},{20,16},{24,28},{28,24},{1,5},{5... | collective-permute-start | bytes 393224 | tf_op jit(solution)/shard_map/ppermute | solution.py:998
  124.4 32.3 %all-to-all-start.3 = ((bf16[8,512,128]{2,1,0:T(8,128)(2,1)}), bf16[8,512,128]{2,1,0:T(8,128)(2,1)S(1)}, u32[]{:S(2)}, u32[]{:S(2)}) async-start(bf16[8,512,128]{2,1,0:T(8,128)(2,1)} %get-tuple-element.135), calls=%async_computation.3 | async-start | bytes 2097152 | tf_op jit(solution)/shard_map/all_to_all | solution.py:1002
  133.1 21.2 %collective-permute-start.27 = (bf16[8,32,1536]{2,1,0:T(8,128)(2,1)}, bf16[8,32,1536]{2,1,0:T(8,128)(2,1)S(1)}, u32[]{:S(2)}, u32[]{:S(2)}) collective-permute-start(bf16[8,32,1536]{2,1,0:T(8,128)(2,1)} %get-tuple-element.124), channel_id=1, source_target_pairs={{0,2},{1,3},{2,0},{3,1},{4,6},{5,7},{6,4},{7,5},{8,10},{9,11},{10,... | collective-permute-start | bytes 2359304 | tf_op jit(solution)/shard_map/ppermute | solution.py:998
  133.7 20.7 %collective-permute-start.24 = (bf16[4,64,1024]{2,1,0:T(8,128)(2,1)S(1)}, bf16[4,64,1024]{2,1,0:T(8,128)(2,1)S(1)}, u32[]{:S(2)}, u32[]{:S(2)}) collective-permute-start(bf16[4,64,1024]{2,1,0:T(8,128)(2,1)S(1)} %copy-done.26), channel_id=1, source_target_pairs={{0,4},{4,0},{8,12},{12,8},{16,20},{20,16},{24,28},{28,24},{1,5},{5... | collective-permute-start | bytes 1572872 | tf_op jit(solution)/shard_map/ppermute | solution.py:998
  156.7 31.6 %all-to-all-start.4 = ((bf16[8,32,1536]{2,1,0:T(8,128)(2,1)}), bf16[8,32,1536]{2,1,0:T(8,128)(2,1)S(1)}, u32[]{:S(2)}, u32[]{:S(2)}) async-start(bf16[8,32,1536]{2,1,0:T(8,128)(2,1)} %shard_map.338.refs_2_.refs_14_.refs_0_), calls=%async_computation.4 | async-start | bytes 1572864 | tf_op jit(solution)/shard_map/all_to_all | solution.py:1002
  178.2 17.8 %collective-permute-start.36 = (bf16[8,32,512]{2,1,0:T(8,128)(2,1)}, bf16[8,32,512]{2,1,0:T(8,128)(2,1)S(1)}, u32[]{:S(2)}, u32[]{:S(2)}) collective-permute-start(bf16[8,32,512]{2,1,0:T(8,128)(2,1)} %get-tuple-element.145), channel_id=1, source_target_pairs={{0,2},{1,3},{2,0},{3,1},{4,6},{5,7},{6,4},{7,5},{8,10},{9,11},{10,... | collective-permute-start | bytes 786440 | tf_op jit(solution)/shard_map/ppermute | solution.py:998
  179.3 16.6 %collective-permute-start.37 = (bf16[8,32,512]{2,1,0:T(8,128)(2,1)}, bf16[8,32,512]{2,1,0:T(8,128)(2,1)S(1)}, u32[]{:S(2)}, u32[]{:S(2)}) collective-permute-start(bf16[8,32,512]{2,1,0:T(8,128)(2,1)} %get-tuple-element.146), channel_id=1, source_target_pairs={{0,3},{1,2},{2,1},{3,0},{4,7},{5,6},{6,5},{7,4},{8,11},{9,10},{10,... | collective-permute-start | bytes 786440 | tf_op jit(solution)/shard_map/ppermute | solution.py:998
  179.3 24.5 %collective-permute-start.32 = (bf16[4,64,1024]{2,1,0:T(8,128)(2,1)}, bf16[4,64,1024]{2,1,0:T(8,128)(2,1)S(1)}, u32[]{:S(2)}, u32[]{:S(2)}) collective-permute-start(bf16[4,64,1024]{2,1,0:T(8,128)(2,1)} %get-tuple-element.139), channel_id=1, source_target_pairs={{0,4},{4,0},{8,12},{12,8},{16,20},{20,16},{24,28},{28,24},{1,5},{5... | collective-permute-start | bytes 1572872 | tf_op jit(solution)/shard_map/ppermute | solution.py:998
  198.0 16.0 %all-to-all-start.5 = ((bf16[8,32,512]{2,1,0:T(8,128)(2,1)}), bf16[8,32,512]{2,1,0:T(8,128)(2,1)S(1)}, u32[]{:S(2)}, u32[]{:S(2)}) async-start(bf16[8,32,512]{2,1,0:T(8,128)(2,1)} %shard_map.344), calls=%async_computation.5 | async-start | bytes 524288 | tf_op jit(solution)/shard_map/all_to_all | solution.py:1002
  205.9 19.8 %collective-permute-start.33 = (bf16[64,1024]{1,0:T(8,128)(2,1)}, bf16[64,1024]{1,0:T(8,128)(2,1)S(1)}, u32[]{:S(2)}, u32[]{:S(2)}) collective-permute-start(bf16[64,1024]{1,0:T(8,128)(2,1)} %get-tuple-element.141), channel_id=1, source_target_pairs={{0,8},{4,12},{8,0},{12,4},{16,24},{20,28},{24,16},{28,20},{1,9},{5... | collective-permute-start | bytes 393224 | tf_op jit(solution)/shard_map/ppermute | solution.py:998
  208.0 17.7 %collective-permute-start.34 = (bf16[64,1024]{1,0:T(8,128)(2,1)}, bf16[64,1024]{1,0:T(8,128)(2,1)S(1)}, u32[]{:S(2)}, u32[]{:S(2)}) collective-permute-start(bf16[64,1024]{1,0:T(8,128)(2,1)} %get-tuple-element.142), channel_id=1, source_target_pairs={{0,16},{4,20},{8,24},{12,28},{16,0},{20,4},{24,8},{28,12},{1,17},{... | collective-permute-start | bytes 393224 | tf_op jit(solution)/shard_map/ppermute | solution.py:998
  210.3 15.3 %collective-permute-start.35 = (bf16[64,1024]{1,0:T(8,128)(2,1)}, bf16[64,1024]{1,0:T(8,128)(2,1)S(1)}, u32[]{:S(2)}, u32[]{:S(2)}) collective-permute-start(bf16[64,1024]{1,0:T(8,128)(2,1)} %get-tuple-element.143), channel_id=1, source_target_pairs={{0,24},{4,28},{8,16},{12,20},{16,8},{20,12},{24,0},{28,4},{1,25},{... | collective-permute-start | bytes 393224 | tf_op jit(solution)/shard_map/ppermute | solution.py:998
  (55 other events, 659.9 us)
where the time goes:
time: 230 us; the launch traced here: 229 us
  waiting for transfers between devices  86.1 us (37%)
  starting transfers between devices  70.7 us (31%)
  Pallas kernels  67.6 us (29%)
  local copies, waits for them, and re-layouts  2.8 us (1%)
    ppermute x41, waiting for transfers between devices, swap(): return lax.ppermute(values, axis, pairs)  77.3 us
    pallas_call x17, Pallas kernels, local_call(): pl.pallas_call(kernel, out_shape=[pltpu.HBM(out.shape, out.dtype) for out...  67.6 us
    ppermute x41, starting transfers between devices, swap(): return lax.ppermute(values, axis, pairs)  42 us
    all_to_all x5, starting transfers between devices, exchange(): return lax.all_to_all(blocks, 'seq', 0, 0)  22.3 us
    all_to_all x1, waiting for transfers between devices, gather_column(): return lax.all_to_all(copies, 'seq', 0, 0, axis_index_groups=groups)  8.41 us
    all_to_all x1, starting transfers between devices, gather_column(): return lax.all_to_all(copies, 'seq', 0, 0, axis_index_groups=groups)  6.33 us
  transfers between devices with their start and end apart: 47, of which 20 were waited for; matrix products, arithmetic and copies ran while one was open for 0% of the time, Pallas kernels for 18%

commit v1 on v0

--- a/solution.py
+++ b/solution.py
@@ -1157,7 +1157,7 @@
     dy_pieces = share_rows([after(block, x_pieces[1]) for block in dy_columns])
     head_columns = share_column(sent_heads)
     head_pieces = share_rows(head_columns)
-    got_second = after(got_second, sent_heads, *dy_pieces[1::2])
+    got_second = after(got_second, head_columns[3], *dy_pieces[1::2])
     second_pieces = share_fsdp(got_second, (*head_pieces[1::2], *dy_pieces[1::2]))
     (
         sent_heads,

time: 230 us -> 228 us (level)
  waiting for transfers between devices: 86.1 us -> 78.2 us
  starting transfers between devices: 70.7 us -> 75.2 us
    ppermute x41, waiting for transfers between devices: 77.3 us -> 69.4 us  [swap(): return lax.ppermute(values, axis, pairs)]
    ppermute x41, starting transfers between devices: 42 us -> 44.6 us  [swap(): return lax.ppermute(values, axis, pairs)]
  transfers between devices with their start and end apart: 47 -> 47, of which waited for: 20 -> 21; matrix products, arithmetic and copies ran while one was open for 0% -> 0% of each run, Pallas kernels for 18% -> 19%
where the time goes in v1:
time: 228 us; the launch traced here: 227 us
  waiting for transfers between devices  78.2 us (34%)
  starting transfers between devices  75.2 us (33%)
  Pallas kernels  67.6 us (30%)
  local copies, waits for them, and re-layouts  3.52 us (2%)
    ppermute x41, waiting for transfers between devices, swap(): return lax.ppermute(values, axis, pairs)  69.4 us
    pallas_call x17, Pallas kernels, local_call(): pl.pallas_call(kernel, out_shape=[pltpu.HBM(out.shape, out.dtype) for out...  67.6 us
    ppermute x41, starting transfers between devices, swap(): return lax.ppermute(values, axis, pairs)  44.6 us
    all_to_all x5, starting transfers between devices, exchange(): return lax.all_to_all(blocks, 'seq', 0, 0)  24.3 us
    all_to_all x1, waiting for transfers between devices, gather_column(): return lax.all_to_all(copies, 'seq', 0, 0, axis_index_groups=groups)  8.42 us
    all_to_all x1, starting transfers between devices, gather_column(): return lax.all_to_all(copies, 'seq', 0, 0, axis_index_groups=groups)  6.33 us
  transfers between devices with their start and end apart: 47, of which 21 were waited for; matrix products, arithmetic and copies ran while one was open for 0% of the time, Pallas kernels for 19%

profile of v1, /device:TPU:0, one launch (start us, length us, event | category | flops | bytes accessed | tf_op | source)
XLA Modules:
  0.0 226.6 jit_solution(18394621639313618055)
XLA Ops:
  3.1 6.3 %all-to-all-start = ((bf16[4,64,1024]{2,1,0:T(8,128)(2,1)}), bf16[4,64,1024]{2,1,0:T(8,128)(2,1)S(1)}, u32[]{:S(2)}, u32[]{:S(2)}) async-start(bf16[4,64,1024]{2,1,0:T(8,128)(2,1)} %get-tuple-element.95), calls=%async_computation | async-start | bytes 1048576 | tf_op jit(solution)/shard_map/all_to_all | solution.py:1018
  15.5 8.4 %all-to-all-done.refs_6_ = bf16[4,64,1024]{2,1,0:T(8,128)(2,1)S(1)} async-done(((bf16[4,64,1024]{2,1,0:T(8,128)(2,1)}), bf16[4,64,1024]{2,1,0:T(8,128)(2,1)S(1)}, u32[]{:S(2)}, u32[]{:S(2)}) %all-to-all-start) | async-done | bytes 524320 | tf_op jit(solution)/shard_map/all_to_all | solution.py:1018
  25.4 3.4 %all-to-all-start.1 = ((bf16[8,32,512]{2,1,0:T(8,128)(2,1)}), bf16[8,32,512]{2,1,0:T(8,128)(2,1)S(1)}, u32[]{:S(2)}, u32[]{:S(2)}) async-start(bf16[8,32,512]{2,1,0:T(8,128)(2,1)} %shard_map.332.refs_5_), calls=%async_computation.1 | async-start | bytes 524288 | tf_op jit(solution)/shard_map/all_to_all | solution.py:1002
  29.4 3.7 %collective-permute-start.9 = (bf16[64,1024]{1,0:T(8,128)(2,1)}, bf16[64,1024]{1,0:T(8,128)(2,1)S(1)}, u32[]{:S(2)}, u32[]{:S(2)}) collective-permute-start(bf16[64,1024]{1,0:T(8,128)(2,1)} %get-tuple-element.105.refs_11_.refs_2_), channel_id=1, source_target_pairs={{0,24},{4,28},{8,16},{12,20},{16,8},{20,12},{24,0},{28,4},{1,25},{... | collective-permute-start | bytes 393224 | tf_op jit(solution)/shard_map/ppermute | solution.py:998
  33.8 7.6 %collective-permute-done.9.refs_17_ = bf16[64,1024]{1,0:T(8,128)(2,1)S(1)} collective-permute-done((bf16[64,1024]{1,0:T(8,128)(2,1)}, bf16[64,1024]{1,0:T(8,128)(2,1)S(1)}, u32[]{:S(2)}, u32[]{:S(2)}) %collective-permute-start.9) | collective-permute-done | bytes 131104 | tf_op jit(solution)/shard_map/ppermute | solution.py:998
  41.4 6.9 %collective-permute-done.8.refs_15_ = bf16[64,1024]{1,0:T(8,128)(2,1)S(1)} collective-permute-done((bf16[64,1024]{1,0:T(8,128)(2,1)}, bf16[64,1024]{1,0:T(8,128)(2,1)S(1)}, u32[]{:S(2)}, u32[]{:S(2)}) %collective-permute-start.8) | collective-permute-done | bytes 131104 | tf_op jit(solution)/shard_map/ppermute | solution.py:998
  49.2 3.5 %all-to-all-start.2 = ((bf16[8,32,1536]{2,1,0:T(8,128)(2,1)}), bf16[8,32,1536]{2,1,0:T(8,128)(2,1)S(1)}, u32[]{:S(2)}, u32[]{:S(2)}) async-start(bf16[8,32,1536]{2,1,0:T(8,128)(2,1)} %get-tuple-element.103), calls=%async_computation.2 | async-start | bytes 1572864 | tf_op jit(solution)/shard_map/all_to_all | solution.py:1002
  54.3 5.5 %collective-permute-done.1.refs_4_.refs_11_ = bf16[8,32,512]{2,1,0:T(8,128)(2,1)S(1)} collective-permute-done((bf16[8,32,512]{2,1,0:T(8,128)(2,1)S(1)}, bf16[8,32,512]{2,1,0:T(8,128)(2,1)S(1)}, u32[]{:S(2)}, u32[]{:S(2)}) %collective-permute-start.1) | collective-permute-done | bytes 262176 | tf_op jit(solution)/shard_map/ppermute | solution.py:998
  65.1 6.0 %shard_map.334 = (bf16[512,1024]{1,0:T(8,128)(2,1)}, f32[8,1024]{1,0:T(8,128)}, bf16[512,384]{1,0:T(8,128)(2,1)}, bf16[512,1024]{1,0:T(8,128)(2,1)}, f32[2,512,512]{2,1,0:T(8,128)}, /*index=5*/bf16[512,128]{1,0:T(8,128)(2,1)}) custom-call(s32[2]{0:T(128)S(1)} %pad_add_fusion.refs_0_, s32[1,3]{1,0:T(1,128)S(1)} %copy-done.4, bf16[8,32,512]{2,1,0:T(8,128)(2,1)} %copy-done.6, ...), custom_call_target="tpu_custom_call" | custom-call | flops 1024 | bytes 1024 | tf_op jit(solution)/shard_map/pallas_call | solution.py:484
  71.0 3.3 %collective-permute-start.10 = (bf16[512,128]{1,0:T(8,128)(2,1)}, bf16[512,128]{1,0:T(8,128)(2,1)S(1)}, u32[]{:S(2)}, u32[]{:S(2)}) collective-permute-start(bf16[512,128]{1,0:T(8,128)(2,1)} %get-tuple-element.104.refs_19_.refs_6_), channel_id=1, source_target_pairs={{0,24},{4,28},{8,16},{12,20},{16,8},{20,12},{24,0},{28,4},{1,25},{... | collective-permute-start | bytes 393224 | tf_op jit(solution)/shard_map/ppermute | solution.py:998
  79.9 3.3 %collective-permute-start.20 = (bf16[512,128]{1,0:T(8,128)(2,1)}, bf16[512,128]{1,0:T(8,128)(2,1)S(1)}, u32[]{:S(2)}, u32[]{:S(2)}) collective-permute-start(bf16[512,128]{1,0:T(8,128)(2,1)} %get-tuple-element.104.refs_19_.refs_6_), channel_id=1, source_target_pairs={{0,16},{4,20},{8,24},{12,28},{16,0},{20,4},{24,8},{28,12},{1,17},{... | collective-permute-start | bytes 393224 | tf_op jit(solution)/shard_map/ppermute | solution.py:998
  99.7 12.8 %shard_map.335 = (bf16[8,512,128]{2,1,0:T(8,128)(2,1)}, bf16[512,512]{1,0:T(8,128)(2,1)}, bf16[512,512]{1,0:T(8,128)(2,1)}, bf16[512,1024]{1,0:T(8,128)(2,1)}, b...) custom-call(s32[2]{0:T(128)S(1)} %pad_add_fusion.refs_0_, ...), custom_call_target="tpu_custom_call" | custom-call | flops 1024 | bytes 1024 | tf_op jit(solution)/shard_map/pallas_call | solution.py:484
  112.5 6.8 %shard_map.336 = (bf16[2,8,32,1536]{3,2,1,0:T(8,128)(2,1)}, bf16[2,8,32,1536]{3,2,1,0:T(8,128)(2,1)}, bf16[2,128,1024]{2,1,0:T(8,128)(2,1)}, bf16[2,128,1024]{2,1,0:T(8,128)(2,1)}) custom-call(s32[2]{0:T(128)S(1)} %pad_add_fusion.refs_0_, bf16[512,1024]{1,0:T(8,128)(2,1)} %get-tuple-element.114.refs_1_, bf16[512,512]{1,0:T(8,128)(2,1)} %get-tuple-element.115.refs_2_, ...), custom_call_target="tpu_custom_call" | custom-call | flops 1024 | bytes 1024 | tf_op jit(solution)/shard_map/pallas_call | solution.py:484
  119.5 5.3 %all-to-all-start.3 = ((bf16[8,512,128]{2,1,0:T(8,128)(2,1)}), bf16[8,512,128]{2,1,0:T(8,128)(2,1)S(1)}, u32[]{:S(2)}, u32[]{:S(2)}) async-start(bf16[8,512,128]{2,1,0:T(8,128)(2,1)} %get-tuple-element.135), calls=%async_computation.3 | async-start | bytes 2097152 | tf_op jit(solution)/shard_map/all_to_all | solution.py:1002
  126.8 3.2 %shard_map.337 = (bf16[8,32,1536]{2,1,0:T(8,128)(2,1)}, bf16[8,32,1536]{2,1,0:T(8,128)(2,1)}, f32[128,1024]{1,0:T(8,128)}, bf16[128,1024]{1,0:T(8,128)(2,1)}) custom-call(bf16[2,8,32,1536]{3,2,1,0:T(8,128)(2,1)} %get-tuple-element.119.refs_0_, bf16[2,8,32,1536]{3,2,1,0:T(8,128)(2,1)S(1)} %collective-permute-done.25.refs_1_, ...), custom_call_target="tpu_custom_call" | custom-call | flops 1024 | bytes 1024 | tf_op jit(solution)/shard_map/pallas_call | solution.py:484
  133.2 17.9 %collective-permute-done.24.refs_2_.refs_1_ = bf16[4,64,1024]{2,1,0:T(8,128)(2,1)S(1)} collective-permute-done((bf16[4,64,1024]{2,1,0:T(8,128)(2,1)S(1)}, bf16[4,64,1024]{2,1,0:T(8,128)(2,1)S(1)}, u32[]{:S(2)}, u32[]{:S(2)}) %collective-permute-start.24) | collective-permute-done | bytes 524320 | tf_op jit(solution)/shard_map/ppermute | solution.py:998
  153.5 6.1 %all-to-all-start.4 = ((bf16[8,32,1536]{2,1,0:T(8,128)(2,1)}), bf16[8,32,1536]{2,1,0:T(8,128)(2,1)S(1)}, u32[]{:S(2)}, u32[]{:S(2)}) async-start(bf16[8,32,1536]{2,1,0:T(8,128)(2,1)} %shard_map.338.refs_2_.refs_14_.refs_0_), calls=%async_computation.4 | async-start | bytes 1572864 | tf_op jit(solution)/shard_map/all_to_all | solution.py:1002
  161.6 8.9 %shard_map.341 = (bf16[8,32,512]{2,1,0:T(8,128)(2,1)}, bf16[8,32,512]{2,1,0:T(8,128)(2,1)}, bf16[8,32,512]{2,1,0:T(8,128)(2,1)}, bf16[8,32,512]{2,1,0:T(8,128)(2...) custom-call(s32[2]{0:T(128)S(1)} %pad_add_fusion.refs_0_, bf16[512,384]{1,0:T(8,128)(2,1)} %get-tuple-element.129.refs_1_, ...), custom_call_target="tpu_custom_call" | custom-call | flops 1024 | bytes 1024 | tf_op jit(solution)/shard_map/pallas_call | solution.py:484
  177.8 4.1 %collective-permute-done.28.refs_6_.refs_5_ = bf16[64,1024]{1,0:T(8,128)(2,1)S(1)} collective-permute-done((bf16[64,1024]{1,0:T(8,128)(2,1)S(1)}, bf16[64,1024]{1,0:T(8,128)(2,1)S(1)}, u32[]{:S(2)}, u32[]{:S(2)}) %collective-permute-start.28) | collective-permute-done | bytes 131104 | tf_op jit(solution)/shard_map/ppermute | solution.py:998
  181.9 3.3 %collective-permute-start.30 = (bf16[64,1024]{1,0:T(8,128)(2,1)S(1)}, bf16[64,1024]{1,0:T(8,128)(2,1)S(1)}, u32[]{:S(2)}, u32[]{:S(2)}) collective-permute-start(bf16[64,1024]{1,0:T(8,128)(2,1)S(1)} %copy-done.33), channel_id=1, source_target_pairs={{0,24},{4,28},{8,16},{12,20},{16,8},{20,12},{24,0},{28,4},{1,25},{... | collective-permute-start | bytes 393224 | tf_op jit(solution)/shard_map/ppermute | solution.py:998
  187.6 5.6 %collective-permute-done.29.refs_7_.refs_6_ = bf16[64,1024]{1,0:T(8,128)(2,1)S(1)} collective-permute-done((bf16[64,1024]{1,0:T(8,128)(2,1)S(1)}, bf16[64,1024]{1,0:T(8,128)(2,1)S(1)}, u32[]{:S(2)}, u32[]{:S(2)}) %collective-permute-start.29) | collective-permute-done | bytes 131104 | tf_op jit(solution)/shard_map/ppermute | solution.py:998
  195.3 5.9 %all-to-all-start.5 = ((bf16[8,32,512]{2,1,0:T(8,128)(2,1)}), bf16[8,32,512]{2,1,0:T(8,128)(2,1)S(1)}, u32[]{:S(2)}, u32[]{:S(2)}) async-start(bf16[8,32,512]{2,1,0:T(8,128)(2,1)} %shard_map.344), calls=%async_computation.5 | async-start | bytes 524288 | tf_op jit(solution)/shard_map/all_to_all | solution.py:1002
  217.7 5.2 %shard_map.346 = (f32[32,3072]{1,0:T(8,128)}, f32[32,3072]{1,0:T(8,128)}, f32[32,3072]{1,0:T(8,128)}, f32[32,1024]{1,0:T(8,128)}, f32[32,1024]{1,0:T(8,128)}, /*...) custom-call(s32[2]{0:T(128)S(1)} %pad_add_fusion.refs_0_, ...), custom_call_target="tpu_custom_call" | custom-call | flops 1024 | bytes 1024 | tf_op jit(solution)/shard_map/pallas_call | solution.py:484
  222.9 3.5 %shard_map.347 = bf16[512,1024]{1,0:T(8,128)(2,1)} custom-call(s32[1,64]{1,0:T(1,128)} %refs_0_.9, bf16[512,1024]{1,0:T(8,128)(2,1)} %bitcast.16, bf16[64,1024]{1,0:T(8,128)(2,1)} %get-tuple-element.105.refs_11_.refs_2_, bf16[64,1024]{1,0:T(8,128)(2,1)} %get-tuple-element.140.refs_1_.refs_3_, bf16[64,1024]{1,0:T(8,128)(2,1)S(1)} %collective-permute-done.33.refs_4_, ...), custom_call_target="tpu_custom_call" | custom-call | flops 1024 | bytes 1024 | tf_op jit(solution)/shard_map/pallas_call | solution.py:484
  (162 shorter events, 78.8 us)
Async XLA Ops:
  3.1 20.8 %all-to-all-start = ((bf16[4,64,1024]{2,1,0:T(8,128)(2,1)}), bf16[4,64,1024]{2,1,0:T(8,128)(2,1)S(1)}, u32[]{:S(2)}, u32[]{:S(2)}) async-start(bf16[4,64,1024]{2,1,0:T(8,128)(2,1)} %get-tuple-element.95), calls=%async_computation | async-start | bytes 1048576 | tf_op jit(solution)/shard_map/all_to_all | solution.py:1018
  13.9 15.0 %collective-permute-start.5 = (bf16[128,1024]{1,0:T(8,128)(2,1)}, bf16[128,1024]{1,0:T(8,128)(2,1)S(1)}, u32[]{:S(2)}, u32[]{:S(2)}) collective-permute-start(bf16[128,1024]{1,0:T(8,128)(2,1)} %get-tuple-element.97.refs_8_.refs_7_), channel_id=1, source_target_pairs={{0,2},{1,3},{2,0},{3,1},{4,6},{5,7},{6,4},{7,5},{8,10},{9,11},{10,... | collective-permute-start | bytes 786440 | tf_op jit(solution)/shard_map/ppermute | solution.py:998
  23.9 24.4 %collective-permute-start.3 = (bf16[4,64,1024]{2,1,0:T(8,128)(2,1)S(1)}, bf16[4,64,1024]{2,1,0:T(8,128)(2,1)S(1)}, u32[]{:S(2)}, u32[]{:S(2)}) collective-permute-start(bf16[4,64,1024]{2,1,0:T(8,128)(2,1)S(1)} %all-to-all-done.refs_6_), channel_id=1, source_target_pairs={{0,4},{4,0},{8,12},{12,8},{16,20},{20,16},{24,28},{28,24},{1,5},{5... | collective-permute-start | bytes 1572872 | tf_op jit(solution)/shard_map/ppermute | solution.py:998
  25.4 22.9 %all-to-all-start.1 = ((bf16[8,32,512]{2,1,0:T(8,128)(2,1)}), bf16[8,32,512]{2,1,0:T(8,128)(2,1)S(1)}, u32[]{:S(2)}, u32[]{:S(2)}) async-start(bf16[8,32,512]{2,1,0:T(8,128)(2,1)} %shard_map.332.refs_5_), calls=%async_computation.1 | async-start | bytes 524288 | tf_op jit(solution)/shard_map/all_to_all | solution.py:1002
  29.4 12.0 %collective-permute-start.9 = (bf16[64,1024]{1,0:T(8,128)(2,1)}, bf16[64,1024]{1,0:T(8,128)(2,1)S(1)}, u32[]{:S(2)}, u32[]{:S(2)}) collective-permute-start(bf16[64,1024]{1,0:T(8,128)(2,1)} %get-tuple-element.105.refs_11_.refs_2_), channel_id=1, source_target_pairs={{0,24},{4,28},{8,16},{12,20},{16,8},{20,12},{24,0},{28,4},{1,25},{... | collective-permute-start | bytes 393224 | tf_op jit(solution)/shard_map/ppermute | solution.py:998
  33.1 15.2 %collective-permute-start.8 = (bf16[64,1024]{1,0:T(8,128)(2,1)}, bf16[64,1024]{1,0:T(8,128)(2,1)S(1)}, u32[]{:S(2)}, u32[]{:S(2)}) collective-permute-start(bf16[64,1024]{1,0:T(8,128)(2,1)} %get-tuple-element.105.refs_11_.refs_2_), channel_id=1, source_target_pairs={{0,16},{4,20},{8,24},{12,28},{16,0},{20,4},{24,8},{28,12},{1,17},{... | collective-permute-start | bytes 393224 | tf_op jit(solution)/shard_map/ppermute | solution.py:998
  33.1 15.2 %collective-permute-start.7 = (bf16[64,1024]{1,0:T(8,128)(2,1)}, bf16[64,1024]{1,0:T(8,128)(2,1)S(1)}, u32[]{:S(2)}, u32[]{:S(2)}) collective-permute-start(bf16[64,1024]{1,0:T(8,128)(2,1)} %get-tuple-element.105.refs_11_.refs_2_), channel_id=1, source_target_pairs={{0,8},{4,12},{8,0},{12,4},{16,24},{20,28},{24,16},{28,20},{1,9},{5... | collective-permute-start | bytes 393224 | tf_op jit(solution)/shard_map/ppermute | solution.py:998
  49.2 29.1 %all-to-all-start.2 = ((bf16[8,32,1536]{2,1,0:T(8,128)(2,1)}), bf16[8,32,1536]{2,1,0:T(8,128)(2,1)S(1)}, u32[]{:S(2)}, u32[]{:S(2)}) async-start(bf16[8,32,1536]{2,1,0:T(8,128)(2,1)} %get-tuple-element.103), calls=%async_computation.2 | async-start | bytes 1572864 | tf_op jit(solution)/shard_map/all_to_all | solution.py:1002
  59.9 14.5 %collective-permute-start.11 = (bf16[64,1024]{1,0:T(8,128)(2,1)S(1)}, bf16[64,1024]{1,0:T(8,128)(2,1)S(1)}, u32[]{:S(2)}, u32[]{:S(2)}) collective-permute-start(bf16[64,1024]{1,0:T(8,128)(2,1)S(1)} %copy-done.15), channel_id=1, source_target_pairs={{0,4},{4,0},{8,12},{12,8},{16,20},{20,16},{24,28},{28,24},{1,5},{5... | collective-permute-start | bytes 393224 | tf_op jit(solution)/shard_map/ppermute | solution.py:998
  61.6 12.8 %collective-permute-start.14 = (bf16[64,1024]{1,0:T(8,128)(2,1)}, bf16[64,1024]{1,0:T(8,128)(2,1)S(1)}, u32[]{:S(2)}, u32[]{:S(2)}) collective-permute-start(bf16[64,1024]{1,0:T(8,128)(2,1)} %copy-done.23), channel_id=1, source_target_pairs={{0,4},{4,0},{8,12},{12,8},{16,20},{20,16},{24,28},{28,24},{1,5},{5... | collective-permute-start | bytes 393224 | tf_op jit(solution)/shard_map/ppermute | solution.py:998
  61.9 12.5 %collective-permute-start.13 = (bf16[64,1024]{1,0:T(8,128)(2,1)}, bf16[64,1024]{1,0:T(8,128)(2,1)S(1)}, u32[]{:S(2)}, u32[]{:S(2)}) collective-permute-start(bf16[64,1024]{1,0:T(8,128)(2,1)} %copy-done.24), channel_id=1, source_target_pairs={{0,4},{4,0},{8,12},{12,8},{16,20},{20,16},{24,28},{28,24},{1,5},{5... | collective-permute-start | bytes 393224 | tf_op jit(solution)/shard_map/ppermute | solution.py:998
  63.7 12.7 %collective-permute-start.12 = (bf16[64,1024]{1,0:T(8,128)(2,1)}, bf16[64,1024]{1,0:T(8,128)(2,1)S(1)}, u32[]{:S(2)}, u32[]{:S(2)}) collective-permute-start(bf16[64,1024]{1,0:T(8,128)(2,1)} %copy-done.25), channel_id=1, source_target_pairs={{0,4},{4,0},{8,12},{12,8},{16,20},{20,16},{24,28},{28,24},{1,5},{5... | collective-permute-start | bytes 393224 | tf_op jit(solution)/shard_map/ppermute | solution.py:998
  78.3 18.2 %collective-permute-start.16 = (bf16[8,32,1536]{2,1,0:T(8,128)(2,1)S(1)}, bf16[8,32,1536]{2,1,0:T(8,128)(2,1)S(1)}, u32[]{:S(2)}, u32[]{:S(2)}) collective-permute-start(bf16[8,32,1536]{2,1,0:T(8,128)(2,1)S(1)} %all-to-all-done.2.refs_3_), channel_id=1, source_target_pairs={{0,2},{1,3},{2,0},{3,1},{4,6},{5,7},{6,4},{7,5},{8,10},{9,11},{10,... | collective-permute-start | bytes 2359304 | tf_op jit(solution)/shard_map/ppermute | solution.py:998
  119.5 34.0 %all-to-all-start.3 = ((bf16[8,512,128]{2,1,0:T(8,128)(2,1)}), bf16[8,512,128]{2,1,0:T(8,128)(2,1)S(1)}, u32[]{:S(2)}, u32[]{:S(2)}) async-start(bf16[8,512,128]{2,1,0:T(8,128)(2,1)} %get-tuple-element.135), calls=%async_computation.3 | async-start | bytes 2097152 | tf_op jit(solution)/shard_map/all_to_all | solution.py:1002
  130.0 21.1 %collective-permute-start.27 = (bf16[8,32,1536]{2,1,0:T(8,128)(2,1)}, bf16[8,32,1536]{2,1,0:T(8,128)(2,1)S(1)}, u32[]{:S(2)}, u32[]{:S(2)}) collective-permute-start(bf16[8,32,1536]{2,1,0:T(8,128)(2,1)} %get-tuple-element.124), channel_id=1, source_target_pairs={{0,2},{1,3},{2,0},{3,1},{4,6},{5,7},{6,4},{7,5},{8,10},{9,11},{10,... | collective-permute-start | bytes 2359304 | tf_op jit(solution)/shard_map/ppermute | solution.py:998
  131.3 19.9 %collective-permute-start.24 = (bf16[4,64,1024]{2,1,0:T(8,128)(2,1)S(1)}, bf16[4,64,1024]{2,1,0:T(8,128)(2,1)S(1)}, u32[]{:S(2)}, u32[]{:S(2)}) collective-permute-start(bf16[4,64,1024]{2,1,0:T(8,128)(2,1)S(1)} %copy-done.30), channel_id=1, source_target_pairs={{0,4},{4,0},{8,12},{12,8},{16,20},{20,16},{24,28},{28,24},{1,5},{5... | collective-permute-start | bytes 1572872 | tf_op jit(solution)/shard_map/ppermute | solution.py:998
  153.5 31.8 %all-to-all-start.4 = ((bf16[8,32,1536]{2,1,0:T(8,128)(2,1)}), bf16[8,32,1536]{2,1,0:T(8,128)(2,1)S(1)}, u32[]{:S(2)}, u32[]{:S(2)}) async-start(bf16[8,32,1536]{2,1,0:T(8,128)(2,1)} %shard_map.338.refs_2_.refs_14_.refs_0_), calls=%async_computation.4 | async-start | bytes 1572864 | tf_op jit(solution)/shard_map/all_to_all | solution.py:1002
  175.2 18.0 %collective-permute-start.36 = (bf16[8,32,512]{2,1,0:T(8,128)(2,1)}, bf16[8,32,512]{2,1,0:T(8,128)(2,1)S(1)}, u32[]{:S(2)}, u32[]{:S(2)}) collective-permute-start(bf16[8,32,512]{2,1,0:T(8,128)(2,1)} %get-tuple-element.145), channel_id=1, source_target_pairs={{0,2},{1,3},{2,0},{3,1},{4,6},{5,7},{6,4},{7,5},{8,10},{9,11},{10,... | collective-permute-start | bytes 786440 | tf_op jit(solution)/shard_map/ppermute | solution.py:998
  176.3 16.9 %collective-permute-start.37 = (bf16[8,32,512]{2,1,0:T(8,128)(2,1)}, bf16[8,32,512]{2,1,0:T(8,128)(2,1)S(1)}, u32[]{:S(2)}, u32[]{:S(2)}) collective-permute-start(bf16[8,32,512]{2,1,0:T(8,128)(2,1)} %get-tuple-element.146), channel_id=1, source_target_pairs={{0,3},{1,2},{2,1},{3,0},{4,7},{5,6},{6,5},{7,4},{8,11},{9,10},{10,... | collective-permute-start | bytes 786440 | tf_op jit(solution)/shard_map/ppermute | solution.py:998
  176.3 24.9 %collective-permute-start.32 = (bf16[4,64,1024]{2,1,0:T(8,128)(2,1)}, bf16[4,64,1024]{2,1,0:T(8,128)(2,1)S(1)}, u32[]{:S(2)}, u32[]{:S(2)}) collective-permute-start(bf16[4,64,1024]{2,1,0:T(8,128)(2,1)} %get-tuple-element.139), channel_id=1, source_target_pairs={{0,4},{4,0},{8,12},{12,8},{16,20},{20,16},{24,28},{28,24},{1,5},{5... | collective-permute-start | bytes 1572872 | tf_op jit(solution)/shard_map/ppermute | solution.py:998
  195.3 16.0 %all-to-all-start.5 = ((bf16[8,32,512]{2,1,0:T(8,128)(2,1)}), bf16[8,32,512]{2,1,0:T(8,128)(2,1)S(1)}, u32[]{:S(2)}, u32[]{:S(2)}) async-start(bf16[8,32,512]{2,1,0:T(8,128)(2,1)} %shard_map.344), calls=%async_computation.5 | async-start | bytes 524288 | tf_op jit(solution)/shard_map/all_to_all | solution.py:1002
  203.2 19.8 %collective-permute-start.33 = (bf16[64,1024]{1,0:T(8,128)(2,1)}, bf16[64,1024]{1,0:T(8,128)(2,1)S(1)}, u32[]{:S(2)}, u32[]{:S(2)}) collective-permute-start(bf16[64,1024]{1,0:T(8,128)(2,1)} %get-tuple-element.141), channel_id=1, source_target_pairs={{0,8},{4,12},{8,0},{12,4},{16,24},{20,28},{24,16},{28,20},{1,9},{5... | collective-permute-start | bytes 393224 | tf_op jit(solution)/shard_map/ppermute | solution.py:998
  205.2 17.7 %collective-permute-start.34 = (bf16[64,1024]{1,0:T(8,128)(2,1)}, bf16[64,1024]{1,0:T(8,128)(2,1)S(1)}, u32[]{:S(2)}, u32[]{:S(2)}) collective-permute-start(bf16[64,1024]{1,0:T(8,128)(2,1)} %get-tuple-element.142), channel_id=1, source_target_pairs={{0,16},{4,20},{8,24},{12,28},{16,0},{20,4},{24,8},{28,12},{1,17},{... | collective-permute-start | bytes 393224 | tf_op jit(solution)/shard_map/ppermute | solution.py:998
  207.6 15.3 %collective-permute-start.35 = (bf16[64,1024]{1,0:T(8,128)(2,1)}, bf16[64,1024]{1,0:T(8,128)(2,1)S(1)}, u32[]{:S(2)}, u32[]{:S(2)}) collective-permute-start(bf16[64,1024]{1,0:T(8,128)(2,1)} %get-tuple-element.143), channel_id=1, source_target_pairs={{0,24},{4,28},{8,16},{12,20},{16,8},{20,12},{24,0},{28,4},{1,25},{... | collective-permute-start | bytes 393224 | tf_op jit(solution)/shard_map/ppermute | solution.py:998
  (59 other events, 645.1 us)
